TPU v7x, 128 devices: a whole 4x4x4 slice. The times are simulated.
128 devices in a mesh: shard: 16 (over x, z), blk: 8 (over y, core).
Axes of the slice: x: 4, y: 4, z: 4, core: 2. Of those that a mesh axis runs over, the one named last changes fastest.
Arguments:
- codes: int32 [131072, 128], P(('shard', 'blk')), may hold values from 0 to 255
- cluster_ids: int32 [131072], P(('shard', 'blk')), may hold values from 0 to 1023, as said below
- cluster_owner: int32 [1024], replicated, may hold values from 0 to 15, as said below
- left_pair: int32 [1024], replicated, may hold values from 0 to 7
- codebook: bfloat16 [128, 256, 8], replicated, may hold values from -6 to 6
Outputs:
- within_max: float32 [131072], P(('shard', 'blk'))
- neighbour_max: float32 [131072], P(('shard', 'blk'))
Inputs may be any that keep to these rules, and one draw needn't show every extreme that they name: `cluster_ids`: row r (of device block (r // 1024)) belongs to a cluster of column (r // 1024) % 8, that is an id from column * 128 up to (column + 1) * 128 - 1. In each aligned block of 1024 rows at most 128 rows belong to clusters of any one owner; in every column one owner receives exactly 128 rows from each of the column's 16 blocks. `cluster_owner`: within each column of 128 consecutive clusters every owner owns exactly 8 clusters.
All inputs are finite; a program needn't handle non-finite values.
Results may differ from a plain program's by a relative error of at most 0.0015.
Values may be sent and summed in bfloat16 or wider, within the bound.
No kernel may reach another device: no remote copies, remote signals or barrier semaphores. Data moves between devices by JAX's collectives and lax.ppermute only.
A program may use at most 64 MiB of HBM per device.

v0:
```python
import jax
import jax.numpy as jnp
from jax import lax
from jax.sharding import PartitionSpec as P

EMB = 1024
SUBQ = 128
CODES_K = 256
CPD = 8


norm_epsilon = 1e-06


def from_behind(x, axis, by):
    peers = lax.axis_size(axis)
    return lax.ppermute(x, axis, [(i, (i + by) % peers) for i in range(peers)])


def lookup_small(lookup_keys, small_table):
    entries = jnp.arange(small_table.shape[0], dtype=jnp.int32)
    picked = jnp.where(lookup_keys[:, None] == entries[None, :], small_table[None, :], 0)
    return jnp.sum(picked, axis=1)


def decode_unit(code_rows, codebook):
    row_count = code_rows.shape[0]
    height = min(128, row_count)
    centroid_ids = jnp.arange(CODES_K, dtype=jnp.int32)

    def decode_block(block_codes):
        onehot = (block_codes[:, :, None] == centroid_ids[None, None, :]).astype(jnp.bfloat16)
        parts = jnp.einsum("rmk,mks->rms", onehot, codebook, preferred_element_type=jnp.float32)
        decoded = parts.reshape(height, EMB)
        scale = lax.rsqrt(jnp.sum(decoded * decoded, axis=1, keepdims=True) + norm_epsilon)
        return (decoded * scale).astype(jnp.bfloat16)

    blocks = code_rows.reshape(row_count // height, height, SUBQ)
    return lax.map(decode_block, blocks).reshape(row_count, EMB)


def column_tables(cluster_owner, left_pair, column, owner_index, span):
    owner_col = lax.dynamic_slice_in_dim(cluster_owner, column * span, span)
    pair_col = lax.dynamic_slice_in_dim(left_pair, column * span, span)
    places = jnp.arange(span, dtype=jnp.int32)
    same_owner = owner_col[:, None] == owner_col[None, :]
    earlier = places[None, :] < places[:, None]
    slot_table = jnp.sum(same_owner & earlier, axis=1)
    slots_here = jnp.arange(CPD, dtype=jnp.int32)
    chosen = (owner_col[None, :] == owner_index) & (slot_table[None, :] == slots_here[:, None])
    partner = jnp.sum(jnp.where(chosen, pair_col[None, :], 0), axis=1)
    return (owner_col, slot_table, partner)


def masked_scores(own_embeds, own_keys, other_embeds, other_keys, exclude_self):
    total = own_embeds.shape[0]
    other_total = other_embeds.shape[0]
    height = min(512, total)
    other_places = jnp.arange(other_total, dtype=jnp.int32)

    def one_step(column_best, step_index):
        offset = step_index * height
        piece = lax.dynamic_slice_in_dim(own_embeds, offset, height, 0)
        piece_keys = lax.dynamic_slice_in_dim(own_keys, offset, height, 0)
        scores = lax.dot_general(
            piece, other_embeds, (((1,), (1,)), ((), ())), preferred_element_type=jnp.float32
        )
        linked = (piece_keys[:, None] == other_keys[None, :]) & (other_keys[None, :] >= 0)
        if exclude_self:
            own_places = offset + jnp.arange(height, dtype=jnp.int32)
            linked = linked & (own_places[:, None] != other_places[None, :])
        masked = jnp.where(linked, scores, -1.0)
        return (jnp.maximum(column_best, jnp.max(masked, axis=0)), jnp.max(masked, axis=1))

    initial = jnp.full((other_total,), -1.0, jnp.float32)
    column_best, row_best = lax.scan(
        one_step, initial, jnp.arange(total // height, dtype=jnp.int32)
    )
    return (row_best.reshape(total), column_best)


def on_device(codes, cluster_ids, cluster_owner, left_pair, codebook):
    row_count = codes.shape[0]
    shard_count = lax.axis_size("shard")
    cycle_count = lax.axis_size("blk")
    shard_index = lax.axis_index("shard")
    cycle_index = lax.axis_index("blk")
    capacity = 2 * row_count // shard_count
    received_count = shard_count * capacity
    span = CPD * shard_count
    owner_col, slot_table, partner_mine = column_tables(
        cluster_owner, left_pair, cycle_index, shard_index, span
    )
    local_ids = cluster_ids - cycle_index * span
    destination = lookup_small(local_ids, owner_col)
    row_slot = lookup_small(local_ids, slot_table)
    owner_ids = jnp.arange(shard_count, dtype=jnp.int32)
    dest_onehot = (destination[:, None] == owner_ids[None, :]).astype(jnp.int32)
    row_ranks = jnp.sum(jnp.cumsum(dest_onehot, axis=0) * dest_onehot, axis=1) - 1
    position = destination * capacity + row_ranks
    slot_places = jnp.arange(received_count, dtype=jnp.int32)
    row_places = jnp.arange(row_count, dtype=jnp.int32)
    matches = position[None, :] == slot_places[:, None]
    source_row = jnp.sum(jnp.where(matches, row_places[None, :], 0), axis=1)
    slot_live = jnp.any(matches, axis=1)
    send_slots = jnp.where(slot_live, jnp.take(row_slot, source_row, axis=0), -1)
    unit_rows = decode_unit(codes, codebook)
    send_embeds = jnp.where(
        slot_live[:, None], jnp.take(unit_rows, source_row, axis=0), jnp.zeros((), jnp.bfloat16)
    )
    got_embeds, got_slots = (
        lax.all_to_all(send_embeds, "shard", split_axis=0, concat_axis=0, tiled=True),
        lax.all_to_all(send_slots, "shard", split_axis=0, concat_axis=0, tiled=True),
    )
    left_embeds, left_slots = from_behind((got_embeds, got_slots), "blk", 1)
    within_best, ignored = masked_scores(got_embeds, got_slots, got_embeds, got_slots, True)
    left_keys = jnp.where(got_slots >= 0, lookup_small(got_slots, partner_mine), -2)
    from_left, unused_best = masked_scores(got_embeds, left_keys, left_embeds, left_slots, False)
    right_embeds, right_slots = from_behind((got_embeds, got_slots), "blk", -1)
    right_column = (cycle_index + 1) % cycle_count
    right_owner, right_table, partner_right = column_tables(
        cluster_owner, left_pair, right_column, shard_index, span
    )
    right_keys = jnp.where(right_slots >= 0, lookup_small(right_slots, partner_right), -2)
    from_right, spare_best = masked_scores(got_embeds, got_slots, right_embeds, right_keys, False)
    neighbour_best = jnp.maximum(from_left, from_right)
    answers = jnp.stack([within_best, neighbour_best], axis=0)
    returned_values = lax.all_to_all(answers, "shard", split_axis=1, concat_axis=1, tiled=True)
    result = jnp.take(returned_values, position, axis=1)
    return (result[0], result[1])


def solution(mesh):
    in_specs = (P(("shard", "blk"), None), P(("shard", "blk")), P(), P(), P())
    out_specs = (P(("shard", "blk")), P(("shard", "blk")))
    return jax.shard_map(
        on_device, mesh=mesh, in_specs=in_specs, out_specs=out_specs, check_vma=False
    )
```

profile of v0, /device:TPU:0, one launch (start us, length us, event | category | flops | bytes accessed | tf_op | source)
XLA Modules:
  0.0 285.5 jit_solution(4382347866169364169)
XLA Ops:
  9.9 8.6 %gather_fusion = s32[2048]{0:T(1024)S(1)} fusion(s32[1024]{0:T(1024)S(1)} %get-tuple-element.176, s32[2048]{0:T(1024)S(1)} %broadcast_clamp_fusion), kind=kCustom, calls=%fused_computation | custom fusion | bytes 24576 | tf_op jit(solution)/shard_map/jit(_take)/gather | solution.py:106
  19.1 8.0 %all-to-all-start = ((s32[16,128,1]{1,2,0:T(1,128)}), s32[16,128,1]{1,2,0:T(1,128)}, u32[]{:S(2)}, u32[]{:S(2)}) async-start(s32[16,128,1]{1,2,0:T(1,128)} %bitcast.12), calls=%async_computation | async-start | bytes 16384 | tf_op jit(solution)/shard_map/all_to_all | solution.py:113
  27.1 55.4 %while.44 = (s32[]{:T(128)}, bf16[8,128,1024]{2,1,0:T(8,128)(2,1)S(1)}, s32[8,128,128]{2,1,0:T(8,128)}, bf16[128,256,8]{1,2,0:T(8,128)(2,1)S(1)}, s32[]{:T(128)}) while((s32[]{:T(128)}, bf16[8,128,1024]{2,1,0:T(8,128)(2,1)S(1)}, s32[8,128,128]{2,1,0:T(8,128)}, bf16[128,256,8]{1,2,0:T(8,128)(2,1)S(1)}, s32[]{:T(128)}) %tuple.94), condition=%wide.region_8.9_spmd.clone, body=%wide.region_6.8_spmd.clone.sunk | while | flops 71827456 | bytes 3213389 | solution.py:39
  28.1 5.7 %fusion.43 = (f32[128]{0:T(128)S(1)}, f32[128,128,8]{1,2,0:T(8,128)S(1)}) fusion(bf16[128,256,8]{1,2,0:T(8,128)(2,1)S(1)} %get-tuple-element.394, s32[128,128]{0,1:T(8,128)S(1)} %bitcast.91), kind=kOutput, calls=%fused_computation.19.clone.1 | convolution fusion | flops 71565184 | bytes 1114624 | tf_op jit(solution)/shard_map/while/body/eval_jaxpr/rmk,mks->rms/dot_general | solution.py:33
  35.0 5.7 %fusion.43 = (f32[128]{0:T(128)S(1)}, f32[128,128,8]{1,2,0:T(8,128)S(1)}) fusion(bf16[128,256,8]{1,2,0:T(8,128)(2,1)S(1)} %get-tuple-element.394, s32[128,128]{0,1:T(8,128)S(1)} %bitcast.91), kind=kOutput, calls=%fused_computation.19.clone.1 | convolution fusion | flops 71565184 | bytes 1114624 | tf_op jit(solution)/shard_map/while/body/eval_jaxpr/rmk,mks->rms/dot_general | solution.py:33
  41.9 5.7 %fusion.43 = (f32[128]{0:T(128)S(1)}, f32[128,128,8]{1,2,0:T(8,128)S(1)}) fusion(bf16[128,256,8]{1,2,0:T(8,128)(2,1)S(1)} %get-tuple-element.394, s32[128,128]{0,1:T(8,128)S(1)} %bitcast.91), kind=kOutput, calls=%fused_computation.19.clone.1 | convolution fusion | flops 71565184 | bytes 1114624 | tf_op jit(solution)/shard_map/while/body/eval_jaxpr/rmk,mks->rms/dot_general | solution.py:33
  48.8 5.7 %fusion.43 = (f32[128]{0:T(128)S(1)}, f32[128,128,8]{1,2,0:T(8,128)S(1)}) fusion(bf16[128,256,8]{1,2,0:T(8,128)(2,1)S(1)} %get-tuple-element.394, s32[128,128]{0,1:T(8,128)S(1)} %bitcast.91), kind=kOutput, calls=%fused_computation.19.clone.1 | convolution fusion | flops 71565184 | bytes 1114624 | tf_op jit(solution)/shard_map/while/body/eval_jaxpr/rmk,mks->rms/dot_general | solution.py:33
  55.8 5.7 %fusion.43 = (f32[128]{0:T(128)S(1)}, f32[128,128,8]{1,2,0:T(8,128)S(1)}) fusion(bf16[128,256,8]{1,2,0:T(8,128)(2,1)S(1)} %get-tuple-element.394, s32[128,128]{0,1:T(8,128)S(1)} %bitcast.91), kind=kOutput, calls=%fused_computation.19.clone.1 | convolution fusion | flops 71565184 | bytes 1114624 | tf_op jit(solution)/shard_map/while/body/eval_jaxpr/rmk,mks->rms/dot_general | solution.py:33
  62.7 5.7 %fusion.43 = (f32[128]{0:T(128)S(1)}, f32[128,128,8]{1,2,0:T(8,128)S(1)}) fusion(bf16[128,256,8]{1,2,0:T(8,128)(2,1)S(1)} %get-tuple-element.394, s32[128,128]{0,1:T(8,128)S(1)} %bitcast.91), kind=kOutput, calls=%fused_computation.19.clone.1 | convolution fusion | flops 71565184 | bytes 1114624 | tf_op jit(solution)/shard_map/while/body/eval_jaxpr/rmk,mks->rms/dot_general | solution.py:33
  69.6 5.7 %fusion.43 = (f32[128]{0:T(128)S(1)}, f32[128,128,8]{1,2,0:T(8,128)S(1)}) fusion(bf16[128,256,8]{1,2,0:T(8,128)(2,1)S(1)} %get-tuple-element.394, s32[128,128]{0,1:T(8,128)S(1)} %bitcast.91), kind=kOutput, calls=%fused_computation.19.clone.1 | convolution fusion | flops 71565184 | bytes 1114624 | tf_op jit(solution)/shard_map/while/body/eval_jaxpr/rmk,mks->rms/dot_general | solution.py:33
  76.5 5.7 %fusion.43 = (f32[128]{0:T(128)S(1)}, f32[128,128,8]{1,2,0:T(8,128)S(1)}) fusion(bf16[128,256,8]{1,2,0:T(8,128)(2,1)S(1)} %get-tuple-element.394, s32[128,128]{0,1:T(8,128)S(1)} %bitcast.91), kind=kOutput, calls=%fused_computation.19.clone.1 | convolution fusion | flops 71565184 | bytes 1114624 | tf_op jit(solution)/shard_map/while/body/eval_jaxpr/rmk,mks->rms/dot_general | solution.py:33
  82.5 9.7 %gather_fusion.1 = bf16[2048,1024]{1,0:T(8,128)(2,1)} fusion(bf16[1024,1024]{1,0:T(8,128)(2,1)S(1)} %bitcast.89, s32[2048]{0:T(1024)S(1)} %broadcast_clamp_fusion), kind=kCustom, calls=%fused_computation.1 | custom fusion | bytes 8396800 | tf_op jit(solution)/shard_map/jit(_take)/gather | solution.py:109
  96.1 7.2 %all-to-all-start.1 = ((bf16[16,128,1024]{2,1,0:T(8,128)(2,1)}), bf16[16,128,1024]{2,1,0:T(8,128)(2,1)}, u32[]{:S(2)}, u32[]{:S(2)}) async-start(bf16[16,128,1024]{2,1,0:T(8,128)(2,1)} %select_select_fusion), calls=%async_computation.1 | async-start | bytes 8388608 | tf_op jit(solution)/shard_map/all_to_all | solution.py:112
  109.1 48.7 %all-to-all-done.1 = bf16[16,128,1024]{2,1,0:T(8,128)(2,1)} async-done(((bf16[16,128,1024]{2,1,0:T(8,128)(2,1)}), bf16[16,128,1024]{2,1,0:T(8,128)(2,1)}, u32[]{:S(2)}, u32[]{:S(2)}) %all-to-all-start.1) | async-done | bytes 4194336 | tf_op jit(solution)/shard_map/all_to_all | solution.py:112
  160.8 32.9 %while.45 = (s32[]{:T(128)}, f32[4,512]{1,0:T(4,128)S(1)}, s32[4]{0:T(128)S(1)}, s32[2048]{0:T(1024)}, bf16[2048,1024]{1,0:T(8,128)(2,1)}, /*index=5*/s32[]{:T(128)}, s32[1]{0:T(128)}, s32[]{:T(128)}, s32[]{:T(128)}) while((s32[]{:T(128)}, f32[4,512]{1,0:T(4,128)S(1)}, s32[4]{0:T(128)S(1)}, s32[2048]{0:T(1024)}, ...), condition=%wide.region_13.14_spmd.clone, body=%wide.region_11.13_spmd.clone.sunk | while | flops 2153777152 | bytes 5279919 | solution.py:76
  163.6 5.4 %select_reduce_fusion.15 = f32[512]{0:T(512)S(1)} fusion(bf16[2048,1024]{1,0:T(8,128)(2,1)} %get-tuple-element.484, s32[512]{0:T(512)S(1)} %iota_add_fusion.2, s32[2048]{0:T(1024)} %get-tuple-element.483, s32[512]{0:T(512)S(1)} %dynamic_slice.82, pred[2048]{0:T(1024)(128)(4,1)S(1)} %broadcast_compare_fusion.10, s32[]{:T(128)S(6)} %select_n.214), kind=kOutput, calls=%fused_computation.24.clone.1 | convolution fusion | flops 2153774592 | bytes 5259268 | tf_op jit(solution)/shard_map/while/body/eval_jaxpr/dot_general | solution.py:65
  171.8 5.4 %select_reduce_fusion.15 = f32[512]{0:T(512)S(1)} fusion(bf16[2048,1024]{1,0:T(8,128)(2,1)} %get-tuple-element.484, s32[512]{0:T(512)S(1)} %iota_add_fusion.2, s32[2048]{0:T(1024)} %get-tuple-element.483, s32[512]{0:T(512)S(1)} %dynamic_slice.82, pred[2048]{0:T(1024)(128)(4,1)S(1)} %broadcast_compare_fusion.10, s32[]{:T(128)S(6)} %select_n.214), kind=kOutput, calls=%fused_computation.24.clone.1 | convolution fusion | flops 2153774592 | bytes 5259268 | tf_op jit(solution)/shard_map/while/body/eval_jaxpr/dot_general | solution.py:65
  180.0 5.4 %select_reduce_fusion.15 = f32[512]{0:T(512)S(1)} fusion(bf16[2048,1024]{1,0:T(8,128)(2,1)} %get-tuple-element.484, s32[512]{0:T(512)S(1)} %iota_add_fusion.2, s32[2048]{0:T(1024)} %get-tuple-element.483, s32[512]{0:T(512)S(1)} %dynamic_slice.82, pred[2048]{0:T(1024)(128)(4,1)S(1)} %broadcast_compare_fusion.10, s32[]{:T(128)S(6)} %select_n.214), kind=kOutput, calls=%fused_computation.24.clone.1 | convolution fusion | flops 2153774592 | bytes 5259268 | tf_op jit(solution)/shard_map/while/body/eval_jaxpr/dot_general | solution.py:65
  188.3 5.4 %select_reduce_fusion.15 = f32[512]{0:T(512)S(1)} fusion(bf16[2048,1024]{1,0:T(8,128)(2,1)} %get-tuple-element.484, s32[512]{0:T(512)S(1)} %iota_add_fusion.2, s32[2048]{0:T(1024)} %get-tuple-element.483, s32[512]{0:T(512)S(1)} %dynamic_slice.82, pred[2048]{0:T(1024)(128)(4,1)S(1)} %broadcast_compare_fusion.10, s32[]{:T(128)S(6)} %select_n.214), kind=kOutput, calls=%fused_computation.24.clone.1 | convolution fusion | flops 2153774592 | bytes 5259268 | tf_op jit(solution)/shard_map/while/body/eval_jaxpr/dot_general | solution.py:65
  193.8 13.4 %collective-permute-done.1 = bf16[2048,1024]{1,0:T(8,128)(2,1)} collective-permute-done((bf16[2048,1024]{1,0:T(8,128)(2,1)}, bf16[2048,1024]{1,0:T(8,128)(2,1)}, u32[]{:S(2)}, u32[]{:S(2)}) %collective-permute-start.1) | collective-permute-done | bytes 4194336 | tf_op jit(solution)/shard_map/ppermute | solution.py:17
  207.2 26.5 %while.42 = (s32[]{:T(128)}, f32[4,512]{1,0:T(4,128)S(1)}, s32[4]{0:T(128)S(1)}, s32[2048]{0:T(1024)S(1)}, s32[2048]{0:T(1024)S(1)}, /*index=5*/bf16[2048,1024]{...) while((s32[]{:T(128)}, f32[4,512]{1,0:T(4,128)S(1)}, ...), condition=%wide.region_18.19_spmd, body=%wide.region_16.18_spmd.sunk | while | flops 2151679488 | bytes 5275835 | solution.py:76
  233.8 28.8 %while.43 = (s32[]{:T(128)}, f32[4,512]{1,0:T(4,128)S(1)}, s32[4]{0:T(128)S(1)}, s32[2048]{0:T(1024)}, s32[2048]{0:T(1024)S(1)}, /*index=5*/bf16[2048,1024]{1,0:...) while((s32[]{:T(128)}, f32[4,512]{1,0:T(4,128)S(1)}, ...), condition=%wide.region_24.25_spmd, body=%wide.region_22.24_spmd.sunk | while | flops 2151679488 | bytes 5275835 | solution.py:76
  263.2 10.1 %all-to-all-start.2 = ((f32[2,16,128]{2,0,1:T(2,128)}), f32[2,16,128]{2,0,1:T(2,128)S(1)}, u32[]{:S(2)}, u32[]{:S(2)}) async-start(f32[2,16,128]{2,0,1:T(2,128)} %copy.30), calls=%async_computation.2 | async-start | bytes 32768 | tf_op jit(solution)/shard_map/all_to_all | solution.py:128
  273.4 7.6 %all-to-all-done.2 = f32[2,16,128]{2,0,1:T(2,128)S(1)} async-done(((f32[2,16,128]{2,0,1:T(2,128)}), f32[2,16,128]{2,0,1:T(2,128)S(1)}, u32[]{:S(2)}, u32[]{:S(2)}) %all-to-all-start.2) | async-done | bytes 16416 | tf_op jit(solution)/shard_map/all_to_all | solution.py:128
  (165 shorter events, 95.2 us)
Async XLA Ops:
  9.9 17.2 %copy-start = (bf16[128,256,8]{1,2,0:T(8,128)(2,1)S(1)}, bf16[128,256,8]{1,2,0:T(8,128)(2,1)}, u32[]{:S(2)}) copy-start(bf16[128,256,8]{1,2,0:T(8,128)(2,1)} %param.17) | copy-start | bytes 1572868
  19.1 77.0 %all-to-all-start = ((s32[16,128,1]{1,2,0:T(1,128)}), s32[16,128,1]{1,2,0:T(1,128)}, u32[]{:S(2)}, u32[]{:S(2)}) async-start(s32[16,128,1]{1,2,0:T(1,128)} %bitcast.12), calls=%async_computation | async-start | bytes 16384 | tf_op jit(solution)/shard_map/all_to_all | solution.py:113
  96.1 61.7 %all-to-all-start.1 = ((bf16[16,128,1024]{2,1,0:T(8,128)(2,1)}), bf16[16,128,1024]{2,1,0:T(8,128)(2,1)}, u32[]{:S(2)}, u32[]{:S(2)}) async-start(bf16[16,128,1024]{2,1,0:T(8,128)(2,1)} %select_select_fusion), calls=%async_computation.1 | async-start | bytes 8388608 | tf_op jit(solution)/shard_map/all_to_all | solution.py:112
  104.6 89.2 %collective-permute-start = (s32[2048]{0:T(1024)}, s32[2048]{0:T(1024)S(1)}, u32[]{:S(2)}, u32[]{:S(2)}) collective-permute-start(s32[2048]{0:T(1024)} %bitcast.13), channel_id=1, source_target_pairs={{0,1},{1,2},{2,3},{3,4},{4,5},{5,6},{6,7},{7,0},{8,9},{9,10},{10,1... | collective-permute-start | bytes 24584 | tf_op jit(solution)/shard_map/ppermute | solution.py:17
  104.6 53.1 %collective-permute-start.2 = (s32[2048]{0:T(1024)}, s32[2048]{0:T(1024)S(1)}, u32[]{:S(2)}, u32[]{:S(2)}) collective-permute-start(s32[2048]{0:T(1024)} %bitcast.13), channel_id=1, source_target_pairs={{0,7},{1,0},{2,1},{3,2},{4,3},{5,4},{6,5},{7,6},{8,15},{9,8},{10,9... | collective-permute-start | bytes 24584 | tf_op jit(solution)/shard_map/ppermute | solution.py:17
  157.8 49.5 %collective-permute-start.1 = (bf16[2048,1024]{1,0:T(8,128)(2,1)}, bf16[2048,1024]{1,0:T(8,128)(2,1)}, u32[]{:S(2)}, u32[]{:S(2)}) collective-permute-start(bf16[2048,1024]{1,0:T(8,128)(2,1)} %bitcast.19), channel_id=1, source_target_pairs={{0,1},{1,2},{2,3},{3,4},{4,5},{5,6},{6,7},{7,0},{8,9},{9,10},{10,1... | collective-permute-start | bytes 12582920 | tf_op jit(solution)/shard_map/ppermute | solution.py:17
  157.9 75.9 %collective-permute-start.3 = (bf16[2048,1024]{1,0:T(8,128)(2,1)}, bf16[2048,1024]{1,0:T(8,128)(2,1)}, u32[]{:S(2)}, u32[]{:S(2)}) collective-permute-start(bf16[2048,1024]{1,0:T(8,128)(2,1)} %bitcast.19), channel_id=1, source_target_pairs={{0,7},{1,0},{2,1},{3,2},{4,3},{5,4},{6,5},{7,6},{8,15},{9,8},{10,9... | collective-permute-start | bytes 12582920 | tf_op jit(solution)/shard_map/ppermute | solution.py:17
  263.2 17.7 %all-to-all-start.2 = ((f32[2,16,128]{2,0,1:T(2,128)}), f32[2,16,128]{2,0,1:T(2,128)S(1)}, u32[]{:S(2)}, u32[]{:S(2)}) async-start(f32[2,16,128]{2,0,1:T(2,128)} %copy.30), calls=%async_computation.2 | async-start | bytes 32768 | tf_op jit(solution)/shard_map/all_to_all | solution.py:128
where the time goes:
time: 287 us; the launch traced here: 285 us
  matrix products  109 us (38%)
  waiting for transfers between devices  69.7 us (24%)
  local copies, waits for them, and re-layouts  47.6 us (17%)
  starting transfers between devices  31.3 us (11%)
  other arithmetic  18.8 us (7%)
  loops' own time  8.63 us (3%)
    dot_general x12, matrix products, one_step(): lax.dot_general(piece, other_embeds, (((1,), (1,)), ((), ())), preferred_...  62.7 us
    all_to_all x1, waiting for transfers between devices, on_device(): lax.all_to_all(send_embeds, 'shard', split_axis=0, concat_axis=0, tiled=T...  48.7 us
    dot_general x8, matrix products, decode_block(): jnp.einsum('rmk,mks->rms', onehot, codebook, preferred_element_type=jnp.f...  45.8 us
    ppermute x4, waiting for transfers between devices, from_behind(): return lax.ppermute(x, axis, [(i, (i + by) % peers) for i in range(peers)])  13.4 us
    all_to_all x1, starting transfers between devices, on_device(): lax.all_to_all(answers, 'shard', split_axis=1, concat_axis=1, tiled=True)  10.1 us
    gather x1, local copies, waits for them, and re-layouts, on_device(): jnp.take(unit_rows, source_row, axis=0)  9.67 us
    gather x1, local copies, waits for them, and re-layouts, on_device(): jnp.take(row_slot, source_row, axis=0)  8.58 us
    another operation x3, loops' own time, masked_scores(): lax.scan(one_step, initial, jnp.arange(total // height, dtype=jnp.int32))  8.15 us
  transfers between devices with their start and end apart: 7, of which 3 were waited for; matrix products, arithmetic and copies ran while one was open for 44% of the time, Pallas kernels for 0%

commit v1 on v0

v1 whole, which is shorter than its diff:
```python
import functools

import jax
import jax.numpy as jnp
from jax import lax
from jax.experimental import pallas as pl
from jax.experimental.pallas import tpu as pltpu
from jax.sharding import PartitionSpec as P

EMB = 1024
SUBQ = 128
SUB = 8
CODES_K = 256
CPD = 8
LANES = 128
SHARDS = 16
CAP = 128
RECV = SHARDS * CAP
BLOCK = SUBQ + 16
norm_epsilon = 1e-06

VMEM = pl.BlockSpec(memory_space=pltpu.VMEM)
PARAMS = pltpu.CompilerParams(vmem_limit_bytes=48 << 20)


def lane_gather(table, index):
    numbers = lax.GatherDimensionNumbers(
        offset_dims=(),
        collapsed_slice_dims=(1,),
        start_index_map=(1,),
        operand_batching_dims=(0,),
        start_indices_batching_dims=(0,),
    )
    return lax.gather(
        table,
        index[..., None],
        numbers,
        slice_sizes=(1, 1),
        mode=lax.GatherScatterMode.PROMISE_IN_BOUNDS,
    )


def iota(shape, axis):
    return lax.broadcasted_iota(jnp.int32, shape, axis)


def route_kernel(codes_ref, ids_ref, owner_ref, pair_ref, send_ref, dest_ref, rank_ref):
    column = lax.axis_index("blk")
    owner_row = owner_ref[pl.ds(column, 1), :]
    pair_row = pair_ref[pl.ds(column, 1), :]
    owner_sq = jnp.broadcast_to(owner_row, (LANES, LANES))
    sub, lane = iota((LANES, LANES), 0), iota((LANES, LANES), 1)
    same = (owner_sq.T == owner_sq) & (sub < lane)
    slot_row = jnp.sum(same.astype(jnp.int32), axis=0, keepdims=True)
    local = ids_ref[...] - column * LANES
    full = (8, LANES)
    dest = lane_gather(jnp.broadcast_to(owner_row, full), local)
    slot = lane_gather(jnp.broadcast_to(slot_row, full), local)
    pair = lane_gather(jnp.broadcast_to(pair_row, full), local)
    member = jnp.concatenate([(dest == o).astype(jnp.float32) for o in range(SHARDS)], axis=0)
    member = member.astype(jnp.bfloat16)
    before = (sub < lane).astype(jnp.bfloat16)
    in_row = jnp.dot(member, before, preferred_element_type=jnp.float32)
    above = ((sub // 8 == lane // 8) & (lane < sub)).astype(jnp.bfloat16)
    rows_above = jnp.dot(above, member, preferred_element_type=jnp.float32).astype(jnp.bfloat16)
    ones = jnp.ones((LANES, LANES), jnp.bfloat16)
    count = in_row + jnp.dot(rows_above, ones, preferred_element_type=jnp.float32)
    rank = jnp.zeros(full, jnp.float32)
    for o in range(SHARDS):
        rank = jnp.where(dest == o, count[o * 8 : (o + 1) * 8, :], rank)
    rank = rank.astype(jnp.int32)
    dest_ref[...] = dest
    rank_ref[...] = rank
    codes_t = codes_ref[...].astype(jnp.float32).T
    slot_f = (slot + 1).astype(jnp.float32)
    pair_f = (pair + 1).astype(jnp.float32)
    slot_line = jnp.concatenate([slot_f[k : k + 1, :] for k in range(8)], axis=1)
    pair_line = jnp.concatenate([pair_f[k : k + 1, :] for k in range(8)], axis=1)
    tail_row = iota((16, 1024), 0)
    tail = jnp.where(tail_row == 0, slot_line, jnp.where(tail_row == 1, pair_line, 0.0))
    left = jnp.concatenate([codes_t, tail], axis=0).astype(jnp.bfloat16)
    for o in range(SHARDS):
        key = jnp.where(dest == o, rank, -1)
        pick = jnp.concatenate(
            [
                (jnp.broadcast_to(key[k : k + 1, :], (LANES, LANES)) == sub).astype(jnp.float32)
                for k in range(8)
            ],
            axis=1,
        ).astype(jnp.bfloat16)
        block = lax.dot_general(
            left, pick, (((1,), (1,)), ((), ())), preferred_element_type=jnp.float32
        )
        send_ref[o] = block.astype(jnp.bfloat16)


def decode(got_ref, table_ref, norm_ref, scale_ref, ut_ref):
    def add_norms(g, totals):
        totals = list(totals)
        part = pl.ds(pl.multiple_of(g * 16, 16), 16)
        low, high = norm_ref[part, :LANES], norm_ref[part, LANES:]
        for j in range(SHARDS):
            code = got_ref[j, part, :].astype(jnp.int32)
            rest = code & 127
            totals[j] = totals[j] + jnp.where(
                code < LANES, lane_gather(low, rest), lane_gather(high, rest)
            )
        return tuple(totals)

    zero = jnp.zeros((16, LANES), jnp.float32)
    totals = lax.fori_loop(0, SUBQ // 16, add_norms, (zero,) * SHARDS)
    for j in range(SHARDS):
        norm = jnp.sum(totals[j], axis=0, keepdims=True)
        scale_ref[j] = jnp.broadcast_to(lax.rsqrt(norm + norm_epsilon), (16, LANES))

    def one_group(g, carry):
        part = pl.ds(pl.multiple_of(g * 16, 16), 16)
        tables = [(table_ref[g, i, :, :LANES], table_ref[g, i, :, LANES:]) for i in range(SUB)]
        for j in range(SHARDS):
            code = got_ref[j, part, :].astype(jnp.int32).astype(jnp.int16)
            rest = code & 127
            is_low = code < LANES
            scale = scale_ref[j]
            for i in range(SUB):
                value = jnp.where(
                    is_low, lane_gather(tables[i][0], rest), lane_gather(tables[i][1], rest)
                )
                rows = pl.ds(pl.multiple_of(g * 128 + i * 16, 16), 16)
                ut_ref[rows, j * LANES : (j + 1) * LANES] = (
                    value.astype(jnp.float32) * scale
                ).astype(jnp.bfloat16)
        return carry

    lax.fori_loop(0, SUBQ // 16, one_group, 0, unroll=2)


def own_kernel(got_ref, table_ref, norm_ref, ut_ref, u_ref, scale_ref):
    decode(got_ref, table_ref, norm_ref, scale_ref, ut_ref)
    side = 256
    eye = (iota((side, side), 0) == iota((side, side), 1)).astype(jnp.bfloat16)

    def turn(i, carry):
        rows = pl.ds(pl.multiple_of(i * side, side), side)
        for f in range(EMB // side):
            u_ref[rows, f * side : (f + 1) * side] = lax.dot_general(
                eye,
                ut_ref[f * side : (f + 1) * side, rows],
                (((1,), (1,)), ((), ())),
                preferred_element_type=jnp.float32,
            ).astype(jnp.bfloat16)
        return carry

    lax.fori_loop(0, RECV // side, turn, 0)


def spread_keys(got_ref, line, keys_ref):
    for j in range(SHARDS):
        key = got_ref[j, SUBQ : SUBQ + 16, :].astype(jnp.float32)[line : line + 1, :]
        keys_ref[j * LANES : (j + 1) * LANES, :] = jnp.broadcast_to(key, (LANES, LANES)).T


def key_lines(got_ref, line, empty):
    keys = [
        got_ref[j, SUBQ : SUBQ + 16, :].astype(jnp.float32)[line : line + 1, :]
        for j in range(SHARDS)
    ]
    return [jnp.where(key == 0.0, empty, key) for key in keys]


SIDE = 256


def fold_lanes(row_best):
    return jnp.max(row_best.T, axis=0, keepdims=True)


def across_kernel(got_ref, left_ref, table_ref, norm_ref, u_ref, out_ref, ut_ref, scale_ref, keys_ref, line_ref, best_ref):
    decode(left_ref, table_ref, norm_ref, scale_ref, ut_ref)
    spread_keys(got_ref, 1, keys_ref)
    lines = key_lines(left_ref, 0, -1.0)
    for j in range(SHARDS):
        line_ref[j] = jnp.broadcast_to(lines[j], (8, LANES))
    best_ref[...] = jnp.full(best_ref.shape, -1.0, jnp.float32)

    def one_tile(i, carry):
        rows = pl.ds(pl.multiple_of(i * SIDE, SIDE), SIDE)
        key = keys_ref[rows, :].reshape(SIDE // 8, 8, LANES)
        u = u_ref[rows, :]
        row_best = jnp.full((SIDE // 8, 8, LANES), -1.0, jnp.float32)
        for n in range(RECV // SIDE):
            scores = jnp.dot(
                u, ut_ref[:, n * SIDE : (n + 1) * SIDE], preferred_element_type=jnp.float32
            )
            for h in range(SIDE // LANES):
                j = n * (SIDE // LANES) + h
                part = scores[:, h * LANES : (h + 1) * LANES].reshape(SIDE // 8, 8, LANES)
                part = jnp.where(key == line_ref[j][None], part, -1.0)
                row_best = jnp.maximum(row_best, part)
                best_ref[j] = jnp.maximum(best_ref[j], jnp.max(part, axis=0))
        line = fold_lanes(row_best.reshape(SIDE, LANES))
        for h in range(SIDE // LANES):
            out_ref[0, pl.ds(i * (SIDE // LANES) + h, 1), :] = line[:, h * LANES : (h + 1) * LANES]
        return carry

    lax.fori_loop(0, RECV // SIDE, one_tile, 0)
    for j in range(SHARDS):
        out_ref[1, j : j + 1, :] = jnp.max(best_ref[j], axis=0, keepdims=True)


def within_kernel(got_ref, u_ref, ut_ref, out_ref, keys_ref, line_ref, best_ref):
    spread_keys(got_ref, 0, keys_ref)
    lines = key_lines(got_ref, 0, -1.0)
    for j in range(SHARDS):
        line_ref[j] = jnp.broadcast_to(lines[j], (8, LANES))
    best_ref[...] = jnp.full(best_ref.shape, -1.0, jnp.float32)
    sub = iota((SIDE // 8, 8, LANES), 0) * 8 + iota((SIDE // 8, 8, LANES), 1)
    lane = iota((SIDE // 8, 8, LANES), 2)

    def one_tile(i, carry):
        rows = pl.ds(pl.multiple_of(i * SIDE, SIDE), SIDE)
        key = keys_ref[rows, :].reshape(SIDE // 8, 8, LANES)
        u = u_ref[rows, :]

        def one_part(n, row_best):
            scores = jnp.dot(
                u,
                ut_ref[:, pl.ds(pl.multiple_of(n * SIDE, SIDE), SIDE)],
                preferred_element_type=jnp.float32,
            )
            for h in range(SIDE // LANES):
                j = n * (SIDE // LANES) + h
                part = scores[:, h * LANES : (h + 1) * LANES].reshape(SIDE // 8, 8, LANES)
                ok = (key == line_ref[j][None]) & (sub + i * SIDE != lane + j * LANES)
                part = jnp.where(ok, part, -1.0)
                row_best = jnp.maximum(row_best, part)
                best_ref[j] = jnp.maximum(best_ref[j], jnp.max(part, axis=0))
            return row_best

        row_best = jnp.full((SIDE // 8, 8, LANES), -1.0, jnp.float32)
        row_best = lax.fori_loop(i, RECV // SIDE, one_part, row_best)
        line = fold_lanes(row_best.reshape(SIDE, LANES))
        for h in range(SIDE // LANES):
            out_ref[pl.ds(i * (SIDE // LANES) + h, 1), :] = line[:, h * LANES : (h + 1) * LANES]
        return carry

    lax.fori_loop(0, RECV // SIDE, one_tile, 0)
    for j in range(SHARDS):
        out_ref[j : j + 1, :] = jnp.maximum(
            out_ref[j : j + 1, :], jnp.max(best_ref[j], axis=0, keepdims=True)
        )


def pick_kernel(got_ref, dest_ref, rank_ref, within_ref, near_ref):
    dest, rank = dest_ref[...], rank_ref[...]
    within = jnp.zeros((8, LANES), jnp.float32)
    near = within
    for o in range(SHARDS):
        here = dest == o
        first = jnp.broadcast_to(got_ref[o, 0:1, :], (8, LANES))
        second = jnp.broadcast_to(got_ref[o, 1:2, :], (8, LANES))
        within = jnp.where(here, lane_gather(first, rank), within)
        near = jnp.where(here, lane_gather(second, rank), near)
    within_ref[...] = within
    near_ref[...] = near


def kernel_call(body, shapes, count, scratch=(), name=None, flops=0):
    return pl.pallas_call(
        body,
        out_shape=shapes,
        in_specs=[VMEM] * count,
        out_specs=[VMEM] * len(shapes),
        scratch_shapes=list(scratch),
        compiler_params=PARAMS,
        name=name,
        cost_estimate=pl.CostEstimate(flops=flops, bytes_accessed=1 << 20, transcendentals=0),
    )


def shape(dims, kind):
    return jax.ShapeDtypeStruct(dims, kind)


bf16, f32, i32 = jnp.bfloat16, jnp.float32, jnp.int32
K_ROUTE = (route_kernel, [shape((SHARDS, BLOCK, LANES), bf16), shape((8, LANES), i32), shape((8, LANES), i32)], 4)
K_OWN = (own_kernel, [shape((EMB, RECV), bf16), shape((RECV, EMB), bf16)], 3, [pltpu.VMEM((SHARDS, 16, LANES), f32)])
K_ACROSS = (
    across_kernel,
    [shape((2, SHARDS, LANES), f32)],
    5,
    [
        pltpu.VMEM((EMB, RECV), bf16),
        pltpu.VMEM((SHARDS, 16, LANES), f32),
        pltpu.VMEM((RECV, LANES), f32),
        pltpu.VMEM((SHARDS, 8, LANES), f32),
        pltpu.VMEM((SHARDS, 8, LANES), f32),
    ],
)
K_WITHIN = (
    within_kernel,
    [shape((SHARDS, LANES), f32)],
    3,
    [
        pltpu.VMEM((RECV, LANES), f32),
        pltpu.VMEM((SHARDS, 8, LANES), f32),
        pltpu.VMEM((SHARDS, 8, LANES), f32),
    ],
)
K_PICK = (pick_kernel, [shape((8, LANES), f32), shape((8, LANES), f32)], 3)


def from_behind(x, axis, by):
    peers = lax.axis_size(axis)
    return lax.ppermute(x, axis, [(i, (i + by) % peers) for i in range(peers)])


def tables_of(codebook):
    turned = jnp.swapaxes(codebook, 1, 2)
    squares = turned.astype(f32)
    norms = jnp.sum(squares * squares, axis=1)
    table = turned.reshape(SUBQ // 16, 16, SUB, CODES_K).transpose(0, 2, 1, 3)
    return table, norms


def on_device(codes, cluster_ids, cluster_owner, left_pair, codebook):
    send, dest, rank = kernel_call(*K_ROUTE, name="route", flops=1 << 30)(
        codes,
        cluster_ids.reshape(8, LANES),
        cluster_owner.reshape(8, LANES),
        left_pair.reshape(8, LANES),
    )
    table, norms = tables_of(codebook)
    got = lax.all_to_all(send, "shard", split_axis=0, concat_axis=0, tiled=True)
    left = from_behind(got, "blk", 1)
    ut, u = kernel_call(*K_OWN, name="own", flops=8 << 30)(got, table, norms)
    (crossed,) = kernel_call(*K_ACROSS, name="across", flops=16 << 30)(got, left, table, norms, u)
    from_right = from_behind(crossed[1], "blk", -1)
    (within,) = kernel_call(*K_WITHIN, name="within", flops=8 << 30)(got, u, ut)
    near = jnp.maximum(crossed[0], from_right)
    answers = jnp.stack([within, near], axis=1)
    back = lax.all_to_all(answers, "shard", split_axis=0, concat_axis=0, tiled=True)
    within_max, near_max = kernel_call(*K_PICK, name="pick")(back, dest, rank)
    return within_max.reshape(-1), near_max.reshape(-1)


def solution(mesh):
    in_specs = (P(("shard", "blk"), None), P(("shard", "blk")), P(), P(), P())
    out_specs = (P(("shard", "blk")), P(("shard", "blk")))
    return jax.shard_map(
        on_device, mesh=mesh, in_specs=in_specs, out_specs=out_specs, check_vma=False
    )
```

time: 287 us -> 86.7 us (0.30)
  matrix products: 109 us -> 0 us
  waiting for transfers between devices: 69.7 us -> 11.5 us
  Pallas kernels: 0 us -> 44.2 us
  local copies, waits for them, and re-layouts: 47.6 us -> 7.36 us
  starting transfers between devices: 31.3 us -> 10.9 us
  other arithmetic: 18.8 us -> 0.34 us
  blocking collectives: 0 us -> 11.2 us
  loops' own time: 8.63 us -> 0 us
    dot_general x20 -> x0, matrix products: 109 us -> none  [the longest x12 62.7 us: one_step(): lax.dot_general(piece, other_embeds, (((1,), (1,)), ((), ())), preferred_...]
    all_to_all x3 -> x1, waiting for transfers between devices: 56.2 us -> 11.4 us  [on_device(): got = lax.all_to_all(send, 'shard', split_axis=0, concat_axis=0, tiled=True)]
    pallas_call x0 -> x5, Pallas kernels: none -> 44.2 us  [the longest x1 16 us: on_device(): kernel_call(*K_ACROSS, name='across', flops=16 << 30)]
    dynamic_slice x41 -> x0, local copies, waits for them, and re-layouts: 22.2 us -> none  [the longest x12 7.55 us: masked_scores(): lax.scan(one_step, initial, jnp.arange(total // height, dtype=jnp.int32))]
    gather x3 -> x0, local copies, waits for them, and re-layouts: 21.1 us -> none  [the longest x1 9.67 us: on_device(): jnp.take(unit_rows, source_row, axis=0)]
    all_to_all x3 -> x1, starting transfers between devices: 25.4 us -> 7.96 us  [on_device(): got = lax.all_to_all(send, 'shard', split_axis=0, concat_axis=0, tiled=True)]
    ppermute x4 -> x2, waiting for transfers between devices: 13.4 us -> 0.01 us  [from_behind(): return lax.ppermute(x, axis, [(i, (i + by) % peers) for i in range(peers)])]
    all_to_all x0 -> x1, blocking collectives: none -> 11.2 us  [on_device(): lax.all_to_all(answers, 'shard', split_axis=0, concat_axis=0, tiled=True)]
  transfers between devices with their start and end apart: 7 -> 3, of which waited for: 3 -> 1; matrix products, arithmetic and copies ran while one was open for 44% -> 0% of each run, Pallas kernels for 0% -> 29%
where the time goes in v1:
time: 86.7 us; the launch traced here: 86.2 us
  Pallas kernels  44.2 us (51%)
  waiting for transfers between devices  11.5 us (13%)
  blocking collectives  11.2 us (13%)
  starting transfers between devices  10.9 us (13%)
  local copies, waits for them, and re-layouts  7.36 us (8%)
    pallas_call x1, Pallas kernels, on_device(): kernel_call(*K_ACROSS, name='across', flops=16 << 30)  16 us
    pallas_call x1, Pallas kernels, on_device(): within, = kernel_call(*K_WITHIN, name='within', flops=8 << 30)(got, u, ut)  15.6 us
    all_to_all x1, waiting for transfers between devices, on_device(): got = lax.all_to_all(send, 'shard', split_axis=0, concat_axis=0, tiled=True)  11.4 us
    all_to_all x1, blocking collectives, on_device(): lax.all_to_all(answers, 'shard', split_axis=0, concat_axis=0, tiled=True)  11.2 us
    pallas_call x1, Pallas kernels, on_device(): ut, u = kernel_call(*K_OWN, name='own', flops=8 << 30)(got, table, norms)  9.41 us
    all_to_all x1, starting transfers between devices, on_device(): got = lax.all_to_all(send, 'shard', split_axis=0, concat_axis=0, tiled=True)  7.96 us
    unnamed x14, local copies, waits for them, and re-layouts  7.25 us
    ppermute x2, starting transfers between devices, from_behind(): return lax.ppermute(x, axis, [(i, (i + by) % peers) for i in range(peers)])  2.96 us
  transfers between devices with their start and end apart: 3, of which 1 were waited for; matrix products, arithmetic and copies ran while one was open for 0% of the time, Pallas kernels for 29%

profile of v1, /device:TPU:0, one launch (start us, length us, event | category | flops | bytes accessed | tf_op | source)
XLA Modules:
  0.0 86.2 jit_solution(10770400859876294549)
XLA Ops:
  0.6 0.0 copy-start
  0.6 1.0 %copy-done = s32[1024,128]{1,0:T(8,128)S(1)} copy-done((s32[1024,128]{1,0:T(8,128)S(1)}, s32[1024,128]{1,0:T(8,128)}, u32[]{:S(2)}) %copy-start) | copy-done | bytes 524312
  1.7 0.0 copy-start.1
  1.7 0.7 copy-done.1
  2.4 0.0 copy-start.2
  2.4 0.7 copy-done.2
  3.1 0.7 copy-done.3
  3.7 2.6 %route.1 = (bf16[16,144,128]{2,1,0:T(8,128)(2,1)}, s32[8,128]{1,0:T(8,128)S(1)}, s32[8,128]{1,0:T(8,128)S(1)}) custom-call(s32[1024,128]{1,0:T(8,128)S(1)} %copy-done, s32[8,128]{1,0:T(8,128)S(1)} %bitcast.23, s32[8,128]{1,0:T(8,128)S(1)} %bitcast.24, s32[8,128]{1,0:T(8,128)S(1)} %bitcast.25), custom_call_target="tpu_custom_call" | custom-call | flops 1073741824 | bytes 1048576 | tf_op jit(solution)/shard_map/route/pallas_call | solution.py:326
  6.3 8.0 %all-to-all-start = ((bf16[16,144,128]{2,1,0:T(8,128)(2,1)}), bf16[16,144,128]{2,1,0:T(8,128)(2,1)S(1)}, u32[]{:S(2)}, u32[]{:S(2)}) async-start(bf16[16,144,128]{2,1,0:T(8,128)(2,1)} %get-tuple-element.9), calls=%async_computation | async-start | bytes 1179648 | tf_op jit(solution)/shard_map/all_to_all | solution.py:333
  14.3 0.0 copy-done.6
  14.3 0.1 copy.9
  14.4 0.3 multiply_reduce_fusion.norm_ref
  14.7 11.4 %all-to-all-done.got_ref = bf16[16,144,128]{2,1,0:T(8,128)(2,1)S(1)} async-done(((bf16[16,144,128]{2,1,0:T(8,128)(2,1)}), bf16[16,144,128]{2,1,0:T(8,128)(2,1)S(1)}, u32[]{:S(2)}, u32[]{:S(2)}) %all-to-all-start) | async-done | bytes 589856 | tf_op jit(solution)/shard_map/all_to_all | solution.py:333
  26.2 0.0 collective-permute-start
  26.2 9.4 %own.1 = (bf16[1024,2048]{1,0:T(8,128)(2,1)S(1)}, bf16[2048,1024]{1,0:T(8,128)(2,1)}) custom-call(bf16[16,144,128]{2,1,0:T(8,128)(2,1)S(1)} %all-to-all-done.got_ref, bf16[8,8,16,256]{3,2,1,0:T(8,128)(2,1)S(1)} %bitcast.20, f32[128,256]{1,0:T(8,128)S(1)} %multiply_reduce_fusion.norm_ref), custom_call_target="tpu_custom_call" | custom-call | flops 8589934592 | bytes 1048576 | tf_op jit(solution)/shard_map/own/pallas_call | solution.py:335
  35.6 2.0 %copy-done.4 = bf16[1024,2048]{1,0:T(8,128)(2,1)} copy-done((bf16[1024,2048]{1,0:T(8,128)(2,1)}, bf16[1024,2048]{1,0:T(8,128)(2,1)S(1)}, u32[]{:S(2)}) %copy-start.4) | copy-done | bytes 4194328
  37.6 0.0 collective-permute-done.left_ref
  37.6 2.2 %copy-done.5 = bf16[2048,1024]{1,0:T(8,128)(2,1)S(1)} copy-done((bf16[2048,1024]{1,0:T(8,128)(2,1)S(1)}, bf16[2048,1024]{1,0:T(8,128)(2,1)}, u32[]{:S(2)}) %copy-start.5) | copy-done | bytes 4194328
  39.8 16.0 %across.1 = f32[2,16,128]{2,1,0:T(8,128)S(1)} custom-call(bf16[16,144,128]{2,1,0:T(8,128)(2,1)S(1)} %all-to-all-done.got_ref, bf16[16,144,128]{2,1,0:T(8,128)(2,1)S(1)} %collective-permute-done.left_ref, bf16[8,8,16,256]{3,2,1,0:T(8,128)(2,1)S(1)} %bitcast.21, f32[128,256]{1,0:T(8,128)S(1)} %multiply_reduce_fusion.norm_ref, bf16[2048,1024]{1,0:T(8,128)(2,1)S(1)} %copy-done.5), custom_call_target="tpu_custom_call" | custom-call | flops 17179869184 | bytes 1048576 | tf_op jit(solution)/shard_map/across/pallas_call | solution.py:336
  55.7 3.0 %collective-permute-start.1 = (f32[16,128]{1,0:T(8,128)S(1)}, f32[16,128]{1,0:T(8,128)S(1)}, u32[]{:S(2)}, u32[]{:S(2)}) collective-permute-start(f32[16,128]{1,0:T(8,128)S(1)} %slice_bitcast_fusion), channel_id=1, source_target_pairs={{0,7},{1,0},{2,1},{3,2},{4,3},{5,4},{6,5},{7,6},{8,15},{9,8},{10,9... | collective-permute-start | bytes 24584 | tf_op jit(solution)/shard_map/ppermute | solution.py:314
  58.7 15.6 %within.1 = f32[16,128]{1,0:T(8,128)S(1)} custom-call(bf16[16,144,128]{2,1,0:T(8,128)(2,1)S(1)} %all-to-all-done.got_ref, bf16[2048,1024]{1,0:T(8,128)(2,1)S(1)} %copy-done.5, bf16[1024,2048]{1,0:T(8,128)(2,1)} %copy-done.4), custom_call_target="tpu_custom_call" | custom-call | flops 8589934592 | bytes 1048576 | tf_op jit(solution)/shard_map/within/pallas_call | solution.py:338
  74.3 0.0 collective-permute-done.1
  74.3 11.2 %all_to_all.10.got_ref = f32[16,2,128]{2,1,0:T(2,128)S(1)} all-to-all(f32[16,2,128]{2,1,0:T(2,128)S(1)} %pad_maximum_fusion), channel_id=1, replica_groups=mesh['shard'=16,'blk'=8] {'shard'}, dimensions={0} | all-to-all | bytes 32768 | tf_op jit(solution)/shard_map/all_to_all | solution.py:341
  85.5 0.7 pick.1
  (7 shorter events, 0.0 us)
Async XLA Ops:
  0.6 1.0 %copy-start = (s32[1024,128]{1,0:T(8,128)S(1)}, s32[1024,128]{1,0:T(8,128)}, u32[]{:S(2)}) copy-start(s32[1024,128]{1,0:T(8,128)} %codes_ref.1) | copy-start | bytes 1572868
  1.7 0.7 copy-start.1
  2.4 0.7 copy-start.2
  3.0 0.7 copy-start.3
  3.7 10.6 %copy-start.6 = (bf16[128,256,8]{1,2,0:T(8,128)(2,1)S(1)}, bf16[128,256,8]{1,2,0:T(8,128)(2,1)}, u32[]{:S(2)}) copy-start(bf16[128,256,8]{1,2,0:T(8,128)(2,1)} %param.9) | copy-start | bytes 1572868
  6.3 19.9 %all-to-all-start = ((bf16[16,144,128]{2,1,0:T(8,128)(2,1)}), bf16[16,144,128]{2,1,0:T(8,128)(2,1)S(1)}, u32[]{:S(2)}, u32[]{:S(2)}) async-start(bf16[16,144,128]{2,1,0:T(8,128)(2,1)} %get-tuple-element.9), calls=%async_computation | async-start | bytes 1179648 | tf_op jit(solution)/shard_map/all_to_all | solution.py:333
  26.2 11.4 %collective-permute-start = (bf16[16,144,128]{2,1,0:T(8,128)(2,1)S(1)}, bf16[16,144,128]{2,1,0:T(8,128)(2,1)S(1)}, u32[]{:S(2)}, u32[]{:S(2)}) collective-permute-start(bf16[16,144,128]{2,1,0:T(8,128)(2,1)S(1)} %all-to-all-done.got_ref), channel_id=1, source_target_pairs={{0,1},{1,2},{2,3},{3,4},{4,5},{5,6},{6,7},{7,0},{8,9},{9,10},{10,1... | collective-permute-start | bytes 1769480 | tf_op jit(solution)/shard_map/ppermute | solution.py:314
  35.6 2.0 %copy-start.4 = (bf16[1024,2048]{1,0:T(8,128)(2,1)}, bf16[1024,2048]{1,0:T(8,128)(2,1)S(1)}, u32[]{:S(2)}) copy-start(bf16[1024,2048]{1,0:T(8,128)(2,1)S(1)} %get-tuple-element.11.ut_ref) | copy-start | bytes 12582916
  37.6 2.2 %copy-start.5 = (bf16[2048,1024]{1,0:T(8,128)(2,1)S(1)}, bf16[2048,1024]{1,0:T(8,128)(2,1)}, u32[]{:S(2)}) copy-start(bf16[2048,1024]{1,0:T(8,128)(2,1)} %get-tuple-element.10.u_ref) | copy-start | bytes 12582916
  55.7 18.5 %collective-permute-start.1 = (f32[16,128]{1,0:T(8,128)S(1)}, f32[16,128]{1,0:T(8,128)S(1)}, u32[]{:S(2)}, u32[]{:S(2)}) collective-permute-start(f32[16,128]{1,0:T(8,128)S(1)} %slice_bitcast_fusion), channel_id=1, source_target_pairs={{0,7},{1,0},{2,1},{3,2},{4,3},{5,4},{6,5},{7,6},{8,15},{9,8},{10,9... | collective-permute-start | bytes 24584 | tf_op jit(solution)/shard_map/ppermute | solution.py:314

commit v2 on v1

v2 whole, which is shorter than its diff:
```python
import functools

import jax
import jax.numpy as jnp
from jax import lax
from jax.experimental import pallas as pl
from jax.experimental.pallas import tpu as pltpu
from jax.sharding import PartitionSpec as P

EMB = 1024
SUBQ = 128
SUB = 8
CODES_K = 256
CPD = 8
LANES = 128
SHARDS = 16
CAP = 128
RECV = SHARDS * CAP
BLOCK = SUBQ + 16
norm_epsilon = 1e-06

VMEM = pl.BlockSpec(memory_space=pltpu.VMEM)


def lane_gather(table, index):
    numbers = lax.GatherDimensionNumbers(
        offset_dims=(),
        collapsed_slice_dims=(1,),
        start_index_map=(1,),
        operand_batching_dims=(0,),
        start_indices_batching_dims=(0,),
    )
    return lax.gather(
        table,
        index[..., None],
        numbers,
        slice_sizes=(1, 1),
        mode=lax.GatherScatterMode.PROMISE_IN_BOUNDS,
    )


def iota(shape, axis):
    return lax.broadcasted_iota(jnp.int32, shape, axis)


def route_kernel(codes_ref, ids_ref, owner_ref, pair_ref, send_ref, dest_ref, rank_ref):
    column = lax.axis_index("blk")
    owner_row = owner_ref[pl.ds(column, 1), :]
    pair_row = pair_ref[pl.ds(column, 1), :]
    owner_sq = jnp.broadcast_to(owner_row, (LANES, LANES))
    sub, lane = iota((LANES, LANES), 0), iota((LANES, LANES), 1)
    same = (owner_sq.T == owner_sq) & (sub < lane)
    slot_row = jnp.sum(same.astype(jnp.int32), axis=0, keepdims=True)
    local = ids_ref[...] - column * LANES
    full = (8, LANES)
    dest = lane_gather(jnp.broadcast_to(owner_row, full), local)
    slot = lane_gather(jnp.broadcast_to(slot_row, full), local)
    pair = lane_gather(jnp.broadcast_to(pair_row, full), local)
    member = jnp.concatenate([(dest == o).astype(jnp.float32) for o in range(SHARDS)], axis=0)
    member = member.astype(jnp.bfloat16)
    before = (sub < lane).astype(jnp.bfloat16)
    in_row = jnp.dot(member, before, preferred_element_type=jnp.float32)
    above = ((sub // 8 == lane // 8) & (lane < sub)).astype(jnp.bfloat16)
    rows_above = jnp.dot(above, member, preferred_element_type=jnp.float32).astype(jnp.bfloat16)
    ones = jnp.ones((LANES, LANES), jnp.bfloat16)
    count = in_row + jnp.dot(rows_above, ones, preferred_element_type=jnp.float32)
    rank = jnp.zeros(full, jnp.float32)
    for o in range(SHARDS):
        rank = jnp.where(dest == o, count[o * 8 : (o + 1) * 8, :], rank)
    rank = rank.astype(jnp.int32)
    dest_ref[...] = dest
    rank_ref[...] = rank
    codes_t = codes_ref[...].astype(jnp.float32).T
    slot_f = (slot + 1).astype(jnp.float32)
    pair_f = (pair + 1).astype(jnp.float32)
    slot_line = jnp.concatenate([slot_f[k : k + 1, :] for k in range(8)], axis=1)
    pair_line = jnp.concatenate([pair_f[k : k + 1, :] for k in range(8)], axis=1)
    tail_row = iota((16, 1024), 0)
    tail = jnp.where(tail_row == 0, slot_line, jnp.where(tail_row == 1, pair_line, 0.0))
    left = jnp.concatenate([codes_t, tail], axis=0).astype(jnp.bfloat16)
    for o in range(SHARDS):
        key = jnp.where(dest == o, rank, -1)
        pick = jnp.concatenate(
            [
                (jnp.broadcast_to(key[k : k + 1, :], (LANES, LANES)) == sub).astype(jnp.float32)
                for k in range(8)
            ],
            axis=1,
        ).astype(jnp.bfloat16)
        block = lax.dot_general(
            left, pick, (((1,), (1,)), ((), ())), preferred_element_type=jnp.float32
        )
        send_ref[o] = block.astype(jnp.bfloat16)


EARLY = 6
SIDE = 256
PER = SIDE // CAP
CHUNKS = RECV // SIDE
GROUP = 16
GROUPS = SUBQ // GROUP


def group_rows(g):
    if isinstance(g, int):
        return slice(g * GROUP, (g + 1) * GROUP)
    return pl.ds(pl.multiple_of(g * GROUP, GROUP), GROUP)


def codes_of(got_ref, block, g):
    return got_ref[block, group_rows(g), :].astype(jnp.int32)


def add_norms(got_ref, norm_ref, block, g, total):
    part = group_rows(g)
    code = codes_of(got_ref, block, g)
    rest = code & 127
    low, high = norm_ref[part, :LANES], norm_ref[part, LANES:]
    return total + jnp.where(code < LANES, lane_gather(low, rest), lane_gather(high, rest))


def scale_of(total):
    norm = jnp.sum(total, axis=0, keepdims=True)
    return jnp.broadcast_to(lax.rsqrt(norm + norm_epsilon), (GROUP, LANES))


def decode_part(got_ref, table_ref, block, g, scale, ut_ref, lanes):
    code = codes_of(got_ref, block, g).astype(jnp.int16)
    rest = code & 127
    is_low = code < LANES
    for i in range(SUB):
        low, high = table_ref[g, i, :, :LANES], table_ref[g, i, :, LANES:]
        value = jnp.where(is_low, lane_gather(low, rest), lane_gather(high, rest))
        rows = group_rows(g * SUB + i)
        ut_ref[rows, lanes] = (value.astype(jnp.float32) * scale).astype(jnp.bfloat16)


def block_lanes(j):
    return slice(j * LANES, (j + 1) * LANES)


def key_row(got_ref, j, line):
    return got_ref[j, SUBQ : SUBQ + 16, :].astype(jnp.float32)[line : line + 1, :]


def spread_keys(got_ref, line, keys_ref):
    for j in range(SHARDS):
        key = key_row(got_ref, j, line)
        keys_ref[j * LANES : (j + 1) * LANES, :] = jnp.broadcast_to(key, (LANES, LANES)).T


def key_line(got_ref, j, line):
    key = key_row(got_ref, j, line)
    return jnp.broadcast_to(jnp.where(key == 0.0, -1.0, key), (8, LANES))


def tiles(x):
    return x.reshape(x.shape[0] // 8, 8, LANES)


def fold_lanes(row_best):
    return jnp.max(row_best.T, axis=0, keepdims=True)


def parts_of(rows):
    half = RECV // 2
    return [slice(r, min(r + half, rows)) for r in range(0, rows, half)]


def scales(got_ref, norm_ref, n):
    totals = [jnp.zeros((GROUP, LANES), jnp.float32)] * PER
    for g in range(GROUPS):
        totals = [add_norms(got_ref, norm_ref, n * PER + h, g, totals[h]) for h in range(PER)]
    return [scale_of(t) for t in totals]


def chunk_scores(n, parts, u_ref, ut, keys_ref, line_of, best_ref, fresh, own, between):
    cols = [jnp.full((8, LANES), -1.0, jnp.float32)] * PER
    for q, rows in enumerate(parts):
        scores = jnp.dot(u_ref[rows, :], ut[...], preferred_element_type=jnp.float32)
        between(q)
        key = tiles(keys_ref[rows, :])
        best = None if fresh(rows) else tiles(best_ref[rows, :])
        for h in range(PER):
            part = tiles(scores[:, h * LANES : (h + 1) * LANES])
            ok = key == line_of(h)[None]
            if own and rows.stop > n * SIDE:
                row = iota(part.shape, 0) * 8 + iota(part.shape, 1)
                ok = ok & (row != iota(part.shape, 2) + (h * LANES + n * SIDE - rows.start))
            part = jnp.where(ok, part, -1.0)
            best = part if best is None else jnp.maximum(best, part)
            cols[h] = jnp.maximum(cols[h], jnp.max(part, axis=0))
        best_ref[rows, :] = best.reshape(rows.stop - rows.start, LANES)
    return [jnp.max(c, axis=0, keepdims=True) for c in cols]


def own_piece(n, got_ref, u_ref, ut_ref, keys_ref, best_ref, out_ref, between):
    cols = chunk_scores(
        n,
        parts_of((n + 1) * SIDE),
        u_ref,
        ut_ref.at[:, n * SIDE : (n + 1) * SIDE],
        keys_ref,
        lambda h: key_line(got_ref, n * PER + h, 0),
        best_ref,
        lambda rows: False,
        True,
        between,
    )
    for h in range(PER):
        j = n * PER + h
        out_ref[j : j + 1, :] = cols[h]


def own_kernel(
    got_ref, table_ref, norm_ref, ut_ref, u_ref, slots_ref, pairs_ref, best_ref, out_ref
):
    eye = (iota((SIDE, SIDE), 0) == iota((SIDE, SIDE), 1)).astype(jnp.bfloat16)

    def decode_chunk(n, groups, scale):
        for g in groups:
            for h in range(PER):
                j = n * PER + h
                decode_part(got_ref, table_ref, j, g, scale[h], ut_ref, block_lanes(j))

    def turn_chunk(n):
        lanes = slice(n * SIDE, (n + 1) * SIDE)
        u_ref[lanes, :] = lax.dot_general(
            eye, ut_ref[:, lanes], (((1,), (1,)), ((), ())), preferred_element_type=jnp.float32
        ).astype(jnp.bfloat16)

    spread_keys(got_ref, 0, slots_ref)
    spread_keys(got_ref, 1, pairs_ref)
    best_ref[...] = jnp.full(best_ref.shape, -1.0, jnp.float32)
    out_ref[...] = jnp.full(out_ref.shape, -1.0, jnp.float32)
    decode_chunk(0, range(GROUPS), scales(got_ref, norm_ref, 0))
    turn_chunk(0)
    for n in range(1, CHUNKS + 1):
        if n < CHUNKS:
            scale = scales(got_ref, norm_ref, n)
            if n - 1 >= EARLY:
                decode_chunk(n, range(GROUPS), scale)
        if n - 1 < EARLY:
            count = len(parts_of(n * SIDE))

            def between(q):
                if n < CHUNKS:
                    decode_chunk(n, range(q * GROUPS // count, (q + 1) * GROUPS // count), scale)

            own_piece(n - 1, got_ref, u_ref, ut_ref, slots_ref, best_ref, out_ref, between)
        if n < CHUNKS:
            turn_chunk(n)


def within_kernel(got_ref, ut_ref, u_ref, slots_ref, best_in, out_in, out_ref, best_ref):
    out_ref[...] = out_in[...]
    best_ref[...] = best_in[...]
    for n in range(EARLY, CHUNKS):
        own_piece(n, got_ref, u_ref, ut_ref, slots_ref, best_ref, out_ref, lambda q: None)
    for j in range(SHARDS):
        row = fold_lanes(best_ref[j * LANES : (j + 1) * LANES, :])
        out_ref[j : j + 1, :] = jnp.maximum(out_ref[j : j + 1, :], row)


def across_kernel(pairs_ref, left_ref, table_ref, norm_ref, u_ref, *rest):
    last = len(rest) == 5
    if last:
        best_in, out_ref, row_ref, ut_a, ut_b = rest
        best_ref = best_in
    else:
        out_ref, best_ref, ut_a, ut_b = rest
    uts = (ut_a, ut_b)
    chunks = left_ref.shape[0] // PER
    parts = parts_of(RECV)

    def decode_chunk(n, groups, scale):
        for g in groups:
            for h in range(PER):
                j = n * PER + h
                decode_part(left_ref, table_ref, j, g, scale[h], uts[n % 2], block_lanes(h))

    decode_chunk(0, range(GROUPS), scales(left_ref, norm_ref, 0))
    for n in range(chunks):
        if n + 1 < chunks:
            scale = scales(left_ref, norm_ref, n + 1)

        def between(q):
            if n + 1 < chunks:
                count = len(parts)
                decode_chunk(n + 1, range(q * GROUPS // count, (q + 1) * GROUPS // count), scale)

        cols = chunk_scores(
            n,
            parts,
            u_ref,
            uts[n % 2],
            pairs_ref,
            lambda h: key_line(left_ref, n * PER + h, 0),
            best_ref,
            lambda rows: n == 0 and not last,
            False,
            between,
        )
        for h in range(PER):
            j = n * PER + h
            out_ref[j : j + 1, :] = cols[h]
    if last:
        for j in range(SHARDS):
            row_ref[j : j + 1, :] = fold_lanes(best_ref[j * LANES : (j + 1) * LANES, :])


def pick_kernel(got_ref, dest_ref, rank_ref, within_ref, near_ref):
    dest, rank = dest_ref[...], rank_ref[...]
    within = jnp.zeros((8, LANES), jnp.float32)
    near = within
    for o in range(SHARDS):
        here = dest == o
        first = jnp.broadcast_to(got_ref[o, 0:1, :], (8, LANES))
        second = jnp.broadcast_to(got_ref[o, 1:2, :], (8, LANES))
        within = jnp.where(here, lane_gather(first, rank), within)
        near = jnp.where(here, lane_gather(second, rank), near)
    within_ref[...] = within
    near_ref[...] = near


def kernel_call(body, shapes, count, scratch=(), name=None, flops=0):
    return pl.pallas_call(
        body,
        out_shape=shapes,
        in_specs=[VMEM] * count,
        out_specs=[VMEM] * len(shapes),
        scratch_shapes=list(scratch),
        compiler_params=pltpu.CompilerParams(vmem_limit_bytes=16 << 20),
        name=name,
        cost_estimate=pl.CostEstimate(flops=flops, bytes_accessed=1 << 20, transcendentals=0),
    )


def shape(dims, kind):
    return jax.ShapeDtypeStruct(dims, kind)


bf16, f32, i32 = jnp.bfloat16, jnp.float32, jnp.int32
K_ROUTE = (
    route_kernel,
    [shape((SHARDS, BLOCK, LANES), bf16), shape((8, LANES), i32), shape((8, LANES), i32)],
    4,
)
K_OWN = (
    own_kernel,
    [
        shape((EMB, RECV), bf16),
        shape((RECV, EMB), bf16),
        shape((RECV, LANES), f32),
        shape((RECV, LANES), f32),
        shape((RECV, LANES), f32),
        shape((SHARDS, LANES), f32),
    ],
    3,
)
UTS = [pltpu.VMEM((EMB, SIDE), bf16)] * 2
HALF = SHARDS // 2
K_FIRST = (across_kernel, [shape((HALF, LANES), f32), shape((RECV, LANES), f32)], 5, UTS)
K_SECOND = (across_kernel, [shape((HALF, LANES), f32), shape((SHARDS, LANES), f32)], 6, UTS)
K_WITHIN = (within_kernel, [shape((SHARDS, LANES), f32)], 6, [pltpu.VMEM((RECV, LANES), f32)])
K_PICK = (pick_kernel, [shape((8, LANES), f32), shape((8, LANES), f32)], 3)


def from_behind(x, axis, by):
    peers = lax.axis_size(axis)
    return lax.ppermute(x, axis, [(i, (i + by) % peers) for i in range(peers)])


def tables_of(codebook):
    turned = jnp.swapaxes(codebook, 1, 2)
    wide = turned.astype(f32)
    norms = jnp.sum(wide * wide, axis=1)
    return turned.reshape(GROUPS, GROUP, SUB, CODES_K).transpose(0, 2, 1, 3), norms


def scores_of(got, left, table, norms):
    ut, u, slots, pairs, best, early = kernel_call(*K_OWN, name="own", flops=8 << 30)(
        got, table, norms
    )
    cols_a, partial = kernel_call(*K_FIRST, name="first", flops=8 << 30)(
        pairs, left[0], table, norms, u
    )
    cols_b, from_left = kernel_call(*K_SECOND, name="second", flops=8 << 30)(
        pairs, left[1], table, norms, u, partial
    )

    def within():
        return kernel_call(*K_WITHIN, name="within", flops=4 << 30)(
            got, ut, u, slots, best, early
        )[0]

    return within, from_left, jnp.concatenate([cols_a, cols_b], axis=0)


def on_device(codes, cluster_ids, cluster_owner, left_pair, codebook):
    send, dest, rank = kernel_call(*K_ROUTE, name="route", flops=1 << 30)(
        codes,
        cluster_ids.reshape(8, LANES),
        cluster_owner.reshape(8, LANES),
        left_pair.reshape(8, LANES),
    )
    table, norms = tables_of(codebook)
    got = lax.all_to_all(send, "shard", split_axis=0, concat_axis=0, tiled=True)
    left = [from_behind(got[h * HALF : (h + 1) * HALF], "blk", 1) for h in range(2)]
    within, from_left, for_left = scores_of(got, left, table, norms)
    from_right = from_behind(for_left, "blk", -1)
    within = within()
    near = jnp.maximum(from_left, from_right)
    answers = jnp.stack([within, near], axis=1)
    back = lax.all_to_all(answers, "shard", split_axis=0, concat_axis=0, tiled=True)
    within_max, near_max = kernel_call(*K_PICK, name="pick")(back, dest, rank)
    return within_max.reshape(-1), near_max.reshape(-1)


def solution(mesh):
    in_specs = (P(("shard", "blk"), None), P(("shard", "blk")), P(), P(), P())
    out_specs = (P(("shard", "blk")), P(("shard", "blk")))
    return jax.shard_map(
        on_device, mesh=mesh, in_specs=in_specs, out_specs=out_specs, check_vma=False
    )
```

time: 86.7 us -> 62.2 us (0.72)
  Pallas kernels: 44.2 us -> 23.9 us
  local copies, waits for them, and re-layouts: 7.36 us -> 3.24 us
    pallas_call x3 -> x4, Pallas kernels: 40.9 us -> 20.6 us  [the longest x1 6.94 us: scores_of(): kernel_call(*K_OWN, name='own', flops=8 << 30)(got, table, norms)]
    unnamed x14 -> x10, local copies, waits for them, and re-layouts: 7.25 us -> 3.1 us
    ppermute x2 -> x3, starting transfers between devices: 2.96 us -> 3.01 us  [from_behind(): return lax.ppermute(x, axis, [(i, (i + by) % peers) for i in range(peers)])]
  transfers between devices with their start and end apart: 3 -> 4, of which waited for: 1 -> 1; matrix products, arithmetic and copies ran while one was open for 0% -> 1% of each run, Pallas kernels for 29% -> 24%
where the time goes in v2:
time: 62.2 us; the launch traced here: 61.8 us
  Pallas kernels  23.9 us (38%)
  waiting for transfers between devices  11.5 us (18%)
  blocking collectives  11.2 us (18%)
  starting transfers between devices  11 us (18%)
  local copies, waits for them, and re-layouts  3.24 us (5%)
  between operations  0.75 us (1%)
    all_to_all x1, waiting for transfers between devices, on_device(): got = lax.all_to_all(send, 'shard', split_axis=0, concat_axis=0, tiled=True)  11.4 us
    all_to_all x1, blocking collectives, on_device(): lax.all_to_all(answers, 'shard', split_axis=0, concat_axis=0, tiled=True)  11.2 us
    all_to_all x1, starting transfers between devices, on_device(): got = lax.all_to_all(send, 'shard', split_axis=0, concat_axis=0, tiled=True)  7.95 us
    pallas_call x1, Pallas kernels, scores_of(): kernel_call(*K_OWN, name='own', flops=8 << 30)(got, table, norms)  6.94 us
    pallas_call x1, Pallas kernels, scores_of(): kernel_call(*K_SECOND, name='second', flops=8 << 30)  5.8 us
    pallas_call x1, Pallas kernels, scores_of(): kernel_call(*K_FIRST, name='first', flops=8 << 30)  5.37 us
    unnamed x10, local copies, waits for them, and re-layouts  3.1 us
    ppermute x3, starting transfers between devices, from_behind(): return lax.ppermute(x, axis, [(i, (i + by) % peers) for i in range(peers)])  3.01 us
  transfers between devices with their start and end apart: 4, of which 1 were waited for; matrix products, arithmetic and copies ran while one was open for 1% of the time, Pallas kernels for 24%

profile of v2, /device:TPU:0, one launch (start us, length us, event | category | flops | bytes accessed | tf_op | source)
XLA Modules:
  0.0 61.8 jit_solution(13808206405586310263)
XLA Ops:
  0.6 0.0 copy-start
  0.6 1.0 %copy-done = s32[1024,128]{1,0:T(8,128)S(1)} copy-done((s32[1024,128]{1,0:T(8,128)S(1)}, s32[1024,128]{1,0:T(8,128)}, u32[]{:S(2)}) %copy-start) | copy-done | bytes 524312
  1.7 0.0 copy-start.1
  1.7 0.7 %copy-done.1 = s32[1024]{0:T(1024)S(1)} copy-done((s32[1024]{0:T(1024)S(1)}, s32[1024]{0:T(1024)}, u32[]{:S(2)}) %copy-start.1) | copy-done | bytes 4120
  2.4 0.7 %copy-done.2 = s32[1024]{0:T(1024)S(1)} copy-done((s32[1024]{0:T(1024)S(1)}, s32[1024]{0:T(1024)}, u32[]{:S(2)}) %copy-start.2) | copy-done | bytes 4120
  3.1 0.7 %copy-done.3 = s32[1024]{0:T(1024)S(1)} copy-done((s32[1024]{0:T(1024)S(1)}, s32[1024]{0:T(1024)}, u32[]{:S(2)}) %copy-start.3) | copy-done | bytes 4120
  3.7 2.6 %route.1 = (bf16[16,144,128]{2,1,0:T(8,128)(2,1)}, s32[8,128]{1,0:T(8,128)S(1)}, s32[8,128]{1,0:T(8,128)S(1)}) custom-call(s32[1024,128]{1,0:T(8,128)S(1)} %copy-done, s32[8,128]{1,0:T(8,128)S(1)} %bitcast.18, s32[8,128]{1,0:T(8,128)S(1)} %bitcast.19, s32[8,128]{1,0:T(8,128)S(1)} %bitcast.20), custom_call_target="tpu_custom_call" | custom-call | flops 1073741824 | bytes 1048576 | tf_op jit(solution)/shard_map/route/pallas_call | solution.py:401
  6.3 8.0 %all-to-all-start = ((bf16[16,144,128]{2,1,0:T(8,128)(2,1)}), bf16[16,144,128]{2,1,0:T(8,128)(2,1)S(1)}, u32[]{:S(2)}, u32[]{:S(2)}) async-start(bf16[16,144,128]{2,1,0:T(8,128)(2,1)} %get-tuple-element.17), calls=%async_computation | async-start | bytes 1179648 | tf_op jit(solution)/shard_map/all_to_all | solution.py:408
  14.3 0.0 copy-done.4
  14.3 0.1 copy.9
  14.4 0.3 multiply_reduce_fusion.norm_ref
  14.7 11.4 %all-to-all-done.got_ref = bf16[16,144,128]{2,1,0:T(8,128)(2,1)S(1)} async-done(((bf16[16,144,128]{2,1,0:T(8,128)(2,1)}), bf16[16,144,128]{2,1,0:T(8,128)(2,1)S(1)}, u32[]{:S(2)}, u32[]{:S(2)}) %all-to-all-start) | async-done | bytes 589856 | tf_op jit(solution)/shard_map/all_to_all | solution.py:408
  26.2 0.0 collective-permute-start.1
  26.3 1.7 %collective-permute-start = (bf16[8,144,128]{2,1,0:T(8,128)(2,1)S(1)}, bf16[8,144,128]{2,1,0:T(8,128)(2,1)S(1)}, u32[]{:S(2)}, u32[]{:S(2)}) collective-permute-start(bf16[8,144,128]{2,1,0:T(8,128)(2,1)S(1)} %get-tuple-element.33), channel_id=1, source_target_pairs={{0,1},{1,2},{2,3},{3,4},{4,5},{5,6},{6,7},{7,0},{8,9},{9,10},{10,1... | collective-permute-start | bytes 884744 | tf_op jit(solution)/shard_map/ppermute | solution.py:371
  27.9 6.9 %own.1 = (bf16[1024,2048]{1,0:T(8,128)(2,1)S(1)}, bf16[2048,1024]{1,0:T(8,128)(2,1)S(1)}, f32[2048,128]{1,0:T(8,128)S(1)}, f32[2048,128]{1,0:T(8,128)S(1)}, f32[...) custom-call(bf16[16,144,128]{2,1,0:T(8,128)(2,1)S(1)} %all-to-all-done.got_ref, bf16[8,8,16,256]{3,2,1,0:T(8,128)(2,1)S(1)} %bitcast.14, ...), custom_call_target="tpu_custom_call" | custom-call | flops 8589934592 | bytes 1048576 | tf_op jit(solution)/shard_map/own/pallas_call | solution.py:382
  34.9 0.0 collective-permute-done.1.left_ref
  34.9 5.4 %first.1 = (f32[8,128]{1,0:T(8,128)S(1)}, f32[2048,128]{1,0:T(8,128)S(1)}) custom-call(f32[2048,128]{1,0:T(8,128)S(1)} %get-tuple-element.23.pairs_ref, bf16[8,144,128]{2,1,0:T(8,128)(2,1)S(1)} %collective-permute-done.1.left_ref, bf16[8,8,16,256]{3,2,1,0:T(8,128)(2,1)S(1)} %bitcast.15, f32[128,256]{1,0:T(8,128)S(1)} %multiply_reduce_fusion.norm_ref, ...), custom_call_target="tpu_custom_call" | custom-call | flops 8589934592 | bytes 1048576 | tf_op jit(solution)/shard_map/first/pallas_call | solution.py:385
  40.3 0.0 collective-permute-done.left_ref
  40.3 5.8 %second.1 = (f32[8,128]{1,0:T(8,128)S(1)}, f32[16,128]{1,0:T(8,128)S(1)}) custom-call(f32[2048,128]{1,0:T(8,128)S(1)} %get-tuple-element.23.pairs_ref, bf16[8,144,128]{2,1,0:T(8,128)(2,1)S(1)} %collective-permute-done.left_ref, bf16[8,8,16,256]{3,2,1,0:T(8,128)(2,1)S(1)} %bitcast.16, f32[128,256]{1,0:T(8,128)S(1)} %multiply_reduce_fusion.norm_ref, ...), custom_call_target="tpu_custom_call" | custom-call | flops 8589934592 | bytes 1048576 | tf_op jit(solution)/shard_map/second/pallas_call | solution.py:388
  46.1 1.3 %collective-permute-start.2 = (f32[16,128]{1,0:T(8,128)S(1)}, f32[16,128]{1,0:T(8,128)S(1)}, u32[]{:S(2)}, u32[]{:S(2)}) collective-permute-start(f32[16,128]{1,0:T(8,128)S(1)} %pad_maximum_fusion.1), channel_id=1, source_target_pairs={{0,7},{1,0},{2,1},{3,2},{4,3},{5,4},{6,5},{7,6},{8,15},{9,8},{10,9... | collective-permute-start | bytes 24584 | tf_op jit(solution)/shard_map/ppermute | solution.py:371
  47.4 2.5 %within.1 = f32[16,128]{1,0:T(8,128)S(1)} custom-call(bf16[16,144,128]{2,1,0:T(8,128)(2,1)S(1)} %all-to-all-done.got_ref, bf16[1024,2048]{1,0:T(8,128)(2,1)S(1)} %get-tuple-element.18.ut_ref, bf16[2048,1024]{1,0:T(8,128)(2,1)S(1)} %get-tuple-element.19.u_ref, f32[2048,128]{1,0:T(8,128)S(1)} %get-tuple-element.20.slots_ref, ...), custom_call_target="tpu_custom_call" | custom-call | flops 4294967296 | bytes 1048576 | tf_op jit(solution)/shard_map/within/pallas_call | solution.py:393
  49.9 0.0 collective-permute-done.2
  50.0 11.2 %all_to_all.10.got_ref = f32[16,2,128]{2,1,0:T(2,128)S(1)} all-to-all(f32[16,2,128]{2,1,0:T(2,128)S(1)} %pad_maximum_fusion), channel_id=1, replica_groups=mesh['shard'=16,'blk'=8] {'shard'}, dimensions={0} | all-to-all | bytes 32768 | tf_op jit(solution)/shard_map/all_to_all | solution.py:415
  61.1 0.7 %pick.1 = (f32[8,128]{1,0:T(8,128)}, f32[8,128]{1,0:T(8,128)}) custom-call(f32[16,2,128]{2,1,0:T(2,128)S(1)} %all_to_all.10.got_ref, s32[8,128]{1,0:T(8,128)S(1)} %get-tuple-element.28.dest_ref, s32[8,128]{1,0:T(8,128)S(1)} %get-tuple-element.29.rank_ref), custom_call_target="tpu_custom_call" | custom-call | bytes 1048576 | tf_op jit(solution)/shard_map/pick/pallas_call | solution.py:416
  (7 shorter events, 0.1 us)
Async XLA Ops:
  0.6 1.0 %copy-start = (s32[1024,128]{1,0:T(8,128)S(1)}, s32[1024,128]{1,0:T(8,128)}, u32[]{:S(2)}) copy-start(s32[1024,128]{1,0:T(8,128)} %codes_ref.1) | copy-start | bytes 1572868
  1.7 0.7 %copy-start.1 = (s32[1024]{0:T(1024)S(1)}, s32[1024]{0:T(1024)}, u32[]{:S(2)}) copy-start(s32[1024]{0:T(1024)} %param.6) | copy-start | bytes 12292
  2.4 0.7 %copy-start.2 = (s32[1024]{0:T(1024)S(1)}, s32[1024]{0:T(1024)}, u32[]{:S(2)}) copy-start(s32[1024]{0:T(1024)} %param.7) | copy-start | bytes 12292
  3.0 0.7 %copy-start.3 = (s32[1024]{0:T(1024)S(1)}, s32[1024]{0:T(1024)}, u32[]{:S(2)}) copy-start(s32[1024]{0:T(1024)} %param.8) | copy-start | bytes 12292
  3.7 10.6 %copy-start.4 = (bf16[128,256,8]{1,2,0:T(8,128)(2,1)S(1)}, bf16[128,256,8]{1,2,0:T(8,128)(2,1)}, u32[]{:S(2)}) copy-start(bf16[128,256,8]{1,2,0:T(8,128)(2,1)} %param.9) | copy-start | bytes 1572868
  6.3 19.9 %all-to-all-start = ((bf16[16,144,128]{2,1,0:T(8,128)(2,1)}), bf16[16,144,128]{2,1,0:T(8,128)(2,1)S(1)}, u32[]{:S(2)}, u32[]{:S(2)}) async-start(bf16[16,144,128]{2,1,0:T(8,128)(2,1)} %get-tuple-element.17), calls=%async_computation | async-start | bytes 1179648 | tf_op jit(solution)/shard_map/all_to_all | solution.py:408
  26.2 8.7 %collective-permute-start.1 = (bf16[8,144,128]{2,1,0:T(8,128)(2,1)S(1)}, bf16[8,144,128]{2,1,0:T(8,128)(2,1)S(1)}, u32[]{:S(2)}, u32[]{:S(2)}) collective-permute-start(bf16[8,144,128]{2,1,0:T(8,128)(2,1)S(1)} %get-tuple-element.32), channel_id=1, source_target_pairs={{0,1},{1,2},{2,3},{3,4},{4,5},{5,6},{6,7},{7,0},{8,9},{9,10},{10,1... | collective-permute-start | bytes 884744 | tf_op jit(solution)/shard_map/ppermute | solution.py:371
  26.3 14.0 %collective-permute-start = (bf16[8,144,128]{2,1,0:T(8,128)(2,1)S(1)}, bf16[8,144,128]{2,1,0:T(8,128)(2,1)S(1)}, u32[]{:S(2)}, u32[]{:S(2)}) collective-permute-start(bf16[8,144,128]{2,1,0:T(8,128)(2,1)S(1)} %get-tuple-element.33), channel_id=1, source_target_pairs={{0,1},{1,2},{2,3},{3,4},{4,5},{5,6},{6,7},{7,0},{8,9},{9,10},{10,1... | collective-permute-start | bytes 884744 | tf_op jit(solution)/shard_map/ppermute | solution.py:371
  46.1 3.8 %collective-permute-start.2 = (f32[16,128]{1,0:T(8,128)S(1)}, f32[16,128]{1,0:T(8,128)S(1)}, u32[]{:S(2)}, u32[]{:S(2)}) collective-permute-start(f32[16,128]{1,0:T(8,128)S(1)} %pad_maximum_fusion.1), channel_id=1, source_target_pairs={{0,7},{1,0},{2,1},{3,2},{4,3},{5,4},{6,5},{7,6},{8,15},{9,8},{10,9... | collective-permute-start | bytes 24584 | tf_op jit(solution)/shard_map/ppermute | solution.py:371

commit v3 on v2

--- a/solution.py
+++ b/solution.py
@@ -43,57 +43,90 @@
     return lax.broadcasted_iota(jnp.int32, shape, axis)
 
 
-def route_kernel(codes_ref, ids_ref, owner_ref, pair_ref, send_ref, dest_ref, rank_ref):
+def route_kernel(
+    codes_hbm, ids_hbm, owner_hbm, pair_hbm, send_hbm, dest_ref, rank_ref,
+    codes_ref, ids_ref, owner_ref, pair_ref, send_ref, in_sem, out_sem,
+):
+    loads = [
+        pltpu.make_async_copy(src, dst, in_sem.at[k])
+        for k, (src, dst) in enumerate(
+            [
+                (owner_hbm, owner_ref),
+                (ids_hbm, ids_ref),
+                (pair_hbm, pair_ref),
+                (codes_hbm, codes_ref),
+            ]
+        )
+    ]
+    for load in loads:
+        load.start()
     column = lax.axis_index("blk")
+    full = (8, LANES)
+    sub, lane = iota((LANES, LANES), 0), iota((LANES, LANES), 1)
+    loads[0].wait()
+    loads[1].wait()
     owner_row = owner_ref[pl.ds(column, 1), :]
-    pair_row = pair_ref[pl.ds(column, 1), :]
-    owner_sq = jnp.broadcast_to(owner_row, (LANES, LANES))
-    sub, lane = iota((LANES, LANES), 0), iota((LANES, LANES), 1)
-    same = (owner_sq.T == owner_sq) & (sub < lane)
-    slot_row = jnp.sum(same.astype(jnp.int32), axis=0, keepdims=True)
     local = ids_ref[...] - column * LANES
-    full = (8, LANES)
     dest = lane_gather(jnp.broadcast_to(owner_row, full), local)
-    slot = lane_gather(jnp.broadcast_to(slot_row, full), local)
-    pair = lane_gather(jnp.broadcast_to(pair_row, full), local)
     member = jnp.concatenate([(dest == o).astype(jnp.float32) for o in range(SHARDS)], axis=0)
     member = member.astype(jnp.bfloat16)
     before = (sub < lane).astype(jnp.bfloat16)
     in_row = jnp.dot(member, before, preferred_element_type=jnp.float32)
     above = ((sub // 8 == lane // 8) & (lane < sub)).astype(jnp.bfloat16)
-    rows_above = jnp.dot(above, member, preferred_element_type=jnp.float32).astype(jnp.bfloat16)
-    ones = jnp.ones((LANES, LANES), jnp.bfloat16)
-    count = in_row + jnp.dot(rows_above, ones, preferred_element_type=jnp.float32)
+    rows_above = jnp.dot(above, member, preferred_element_type=jnp.float32)
+    count = in_row + jnp.sum(rows_above, axis=1, keepdims=True)
     rank = jnp.zeros(full, jnp.float32)
     for o in range(SHARDS):
         rank = jnp.where(dest == o, count[o * 8 : (o + 1) * 8, :], rank)
     rank = rank.astype(jnp.int32)
     dest_ref[...] = dest
     rank_ref[...] = rank
-    codes_t = codes_ref[...].astype(jnp.float32).T
+    owner_sq = jnp.broadcast_to(owner_row, (LANES, LANES))
+    same = (owner_sq.T == owner_sq) & (sub < lane)
+    slot_row = jnp.sum(same.astype(jnp.int32), axis=0, keepdims=True)
+    slot = lane_gather(jnp.broadcast_to(slot_row, full), local)
+    loads[2].wait()
+    pair_row = pair_ref[pl.ds(column, 1), :]
+    pair = lane_gather(jnp.broadcast_to(pair_row, full), local)
     slot_f = (slot + 1).astype(jnp.float32)
     pair_f = (pair + 1).astype(jnp.float32)
     slot_line = jnp.concatenate([slot_f[k : k + 1, :] for k in range(8)], axis=1)
     pair_line = jnp.concatenate([pair_f[k : k + 1, :] for k in range(8)], axis=1)
     tail_row = iota((16, 1024), 0)
     tail = jnp.where(tail_row == 0, slot_line, jnp.where(tail_row == 1, pair_line, 0.0))
+    loads[3].wait()
+    codes_t = codes_ref[...].astype(jnp.float32).T
     left = jnp.concatenate([codes_t, tail], axis=0).astype(jnp.bfloat16)
-    for o in range(SHARDS):
-        key = jnp.where(dest == o, rank, -1)
-        pick = jnp.concatenate(
-            [
+    stores = []
+    for o in range(0, SHARDS, OWNERS):
+        picks = []
+        for p in range(OWNERS):
+            key = jnp.where(dest == o + p, rank, -1)
+            pick = [
                 (jnp.broadcast_to(key[k : k + 1, :], (LANES, LANES)) == sub).astype(jnp.float32)
                 for k in range(8)
-            ],
-            axis=1,
-        ).astype(jnp.bfloat16)
+            ]
+            picks.append(jnp.concatenate(pick, axis=1))
+        pick = jnp.concatenate(picks, axis=0).astype(jnp.bfloat16)
         block = lax.dot_general(
             left, pick, (((1,), (1,)), ((), ())), preferred_element_type=jnp.float32
+        ).astype(jnp.bfloat16)
+        for p in range(OWNERS):
+            send_ref[o + p] = block[:, p * LANES : (p + 1) * LANES]
+        part = pl.ds(o, OWNERS)
+        store = pltpu.make_async_copy(
+            send_ref.at[part], send_hbm.at[part], out_sem.at[o // OWNERS]
         )
-        send_ref[o] = block.astype(jnp.bfloat16)
-
-
-EARLY = 6
+        store.start()
+        stores.append(store)
+    for store in stores:
+        store.wait()
+
+
+OWNERS = 2
+
+
+EARLY = 5
 SIDE = 256
 PER = SIDE // CAP
 CHUNKS = RECV // SIDE
@@ -341,11 +374,6 @@
 
 
 bf16, f32, i32 = jnp.bfloat16, jnp.float32, jnp.int32
-K_ROUTE = (
-    route_kernel,
-    [shape((SHARDS, BLOCK, LANES), bf16), shape((8, LANES), i32), shape((8, LANES), i32)],
-    4,
-)
 K_OWN = (
     own_kernel,
     [
@@ -366,6 +394,32 @@
 K_PICK = (pick_kernel, [shape((8, LANES), f32), shape((8, LANES), f32)], 3)
 
 
+def route_call(*operands):
+    small = pltpu.VMEM((8, LANES), i32)
+    outside = pl.BlockSpec(memory_space=pltpu.HBM)
+    return pl.pallas_call(
+        route_kernel,
+        out_shape=[
+            shape((SHARDS, BLOCK, LANES), bf16),
+            shape((8, LANES), i32),
+            shape((8, LANES), i32),
+        ],
+        in_specs=[outside] * 4,
+        out_specs=[outside, VMEM, VMEM],
+        scratch_shapes=[
+            pltpu.VMEM((SHARDS * 64, LANES), i32),
+            small,
+            small,
+            small,
+            pltpu.VMEM((SHARDS, BLOCK, LANES), bf16),
+            pltpu.SemaphoreType.DMA((4,)),
+            pltpu.SemaphoreType.DMA((SHARDS // OWNERS,)),
+        ],
+        compiler_params=pltpu.CompilerParams(vmem_limit_bytes=16 << 20),
+        name="route",
+    )(*[pltpu.with_memory_space_constraint(x, pltpu.HBM) for x in operands])
+
+
 def from_behind(x, axis, by):
     peers = lax.axis_size(axis)
     return lax.ppermute(x, axis, [(i, (i + by) % peers) for i in range(peers)])
@@ -398,7 +452,7 @@
 
 
 def on_device(codes, cluster_ids, cluster_owner, left_pair, codebook):
-    send, dest, rank = kernel_call(*K_ROUTE, name="route", flops=1 << 30)(
+    send, dest, rank = route_call(
         codes,
         cluster_ids.reshape(8, LANES),
         cluster_owner.reshape(8, LANES),

time: 62.2 us -> 59.4 us (0.955)
  waiting for transfers between devices: 11.5 us -> 9.42 us
  local copies, waits for them, and re-layouts: 3.24 us -> 1.19 us
  other arithmetic: 0.35 us -> 1.4 us
    unnamed x10 -> x0, local copies, waits for them, and re-layouts: 3.1 us -> none
    all_to_all x1, waiting for transfers between devices: 11.4 us -> 9.37 us  [on_device(): got = lax.all_to_all(send, 'shard', split_axis=0, concat_axis=0, tiled=True)]
    pallas_call x1, Pallas kernels: 6.94 us -> 5.61 us  [scores_of(): kernel_call(*K_OWN, name='own', flops=8 << 30)(got, table, norms)]
    reduce_sum x1, other arithmetic: 0.32 us -> 1.37 us  [tables_of(): norms = jnp.sum(wide * wide, axis=1)]
    reshape x1, local copies, waits for them, and re-layouts: 0.1 us -> 1.15 us  [tables_of(): turned.reshape(GROUPS, GROUP, SUB, CODES_K).transpose(0, 2, 1, 3)]
    pallas_call x1, Pallas kernels: 2.49 us -> 3.32 us  [within(): kernel_call(*K_WITHIN, name='within', flops=4 << 30)]
    pallas_call x1, Pallas kernels: 2.6 us -> 3.4 us  [route_call(): pl.pallas_call(route_kernel, out_shape=[shape((SHARDS, BLOCK, LANES), bf1...]
  transfers between devices with their start and end apart: 4 -> 4, of which waited for: 1 -> 1; matrix products, arithmetic and copies ran while one was open for 1% -> 4% of each run, Pallas kernels for 24% -> 24%
where the time goes in v3:
time: 59.4 us; the launch traced here: 59.1 us
  Pallas kernels  24.2 us (41%)
  blocking collectives  11.2 us (19%)
  starting transfers between devices  11 us (19%)
  waiting for transfers between devices  9.42 us (16%)
  other arithmetic  1.4 us (2%)
  local copies, waits for them, and re-layouts  1.19 us (2%)
  between operations  0.72 us (1%)
    all_to_all x1, blocking collectives, on_device(): lax.all_to_all(answers, 'shard', split_axis=0, concat_axis=0, tiled=True)  11.2 us
    all_to_all x1, waiting for transfers between devices, on_device(): got = lax.all_to_all(send, 'shard', split_axis=0, concat_axis=0, tiled=True)  9.37 us
    all_to_all x1, starting transfers between devices, on_device(): got = lax.all_to_all(send, 'shard', split_axis=0, concat_axis=0, tiled=True)  7.98 us
    pallas_call x1, Pallas kernels, scores_of(): kernel_call(*K_SECOND, name='second', flops=8 << 30)  5.8 us
    pallas_call x1, Pallas kernels, scores_of(): kernel_call(*K_OWN, name='own', flops=8 << 30)(got, table, norms)  5.61 us
    pallas_call x1, Pallas kernels, scores_of(): kernel_call(*K_FIRST, name='first', flops=8 << 30)  5.37 us
    pallas_call x1, Pallas kernels, route_call(): pl.pallas_call(route_kernel, out_shape=[shape((SHARDS, BLOCK, LANES), bf1...  3.4 us
    pallas_call x1, Pallas kernels, within(): kernel_call(*K_WITHIN, name='within', flops=4 << 30)  3.32 us
  transfers between devices with their start and end apart: 4, of which 1 were waited for; matrix products, arithmetic and copies ran while one was open for 4% of the time, Pallas kernels for 24%

profile of v3, /device:TPU:0, one launch (start us, length us, event | category | flops | bytes accessed | tf_op | source)
XLA Modules:
  0.0 59.1 jit_solution(2667167935210066122)
XLA Ops:
  0.6 3.4 %route.1 = (bf16[16,144,128]{2,1,0:T(8,128)(2,1)}, s32[8,128]{1,0:T(8,128)S(1)}, s32[8,128]{1,0:T(8,128)S(1)}) custom-call(s32[1024,128]{1,0:T(8,128)} %codes_hbm.1, s32[8,128]{1,0:T(8,128)} %bitcast.20, s32[8,128]{1,0:T(8,128)} %bitcast.21, s32[8,128]{1,0:T(8,128)} %bitcast.22), custom_call_target="tpu_custom_call" | custom-call | tf_op jit(solution)/shard_map/route/pallas_call | solution.py:400
  4.0 8.0 %all-to-all-start = ((bf16[16,144,128]{2,1,0:T(8,128)(2,1)}), bf16[16,144,128]{2,1,0:T(8,128)(2,1)S(1)}, u32[]{:S(2)}, u32[]{:S(2)}) async-start(bf16[16,144,128]{2,1,0:T(8,128)(2,1)} %get-tuple-element.17), calls=%async_computation | async-start | bytes 1179648 | tf_op jit(solution)/shard_map/all_to_all | solution.py:462
  12.0 1.1 %copy.9 = bf16[8,16,8,256]{3,1,2,0:T(8,128)(2,1)S(1)} copy(bf16[8,16,8,256]{3,2,1,0:T(8,128)(2,1)} %bitcast.18) | data formatting | bytes 1048576 | tf_op jit(solution)/shard_map/reshape | solution.py:432
  13.2 1.4 %multiply_reduce_fusion.norm_ref = f32[128,256]{1,0:T(8,128)S(1)} fusion(bf16[128,256,8]{1,2,0:T(8,128)(2,1)} %param.9), kind=kLoop, calls=%fused_computation | loop fusion | flops 753664 | bytes 655360 | tf_op jit(solution)/shard_map/reduce_sum | solution.py:431
  14.5 9.4 %all-to-all-done.got_ref = bf16[16,144,128]{2,1,0:T(8,128)(2,1)S(1)} async-done(((bf16[16,144,128]{2,1,0:T(8,128)(2,1)}), bf16[16,144,128]{2,1,0:T(8,128)(2,1)S(1)}, u32[]{:S(2)}, u32[]{:S(2)}) %all-to-all-start) | async-done | bytes 589856 | tf_op jit(solution)/shard_map/all_to_all | solution.py:462
  24.0 0.0 collective-permute-start.1
  24.0 1.7 %collective-permute-start = (bf16[8,144,128]{2,1,0:T(8,128)(2,1)S(1)}, bf16[8,144,128]{2,1,0:T(8,128)(2,1)S(1)}, u32[]{:S(2)}, u32[]{:S(2)}) collective-permute-start(bf16[8,144,128]{2,1,0:T(8,128)(2,1)S(1)} %get-tuple-element.33), channel_id=1, source_target_pairs={{0,1},{1,2},{2,3},{3,4},{4,5},{5,6},{6,7},{7,0},{8,9},{9,10},{10,1... | collective-permute-start | bytes 884744 | tf_op jit(solution)/shard_map/ppermute | solution.py:425
  25.7 5.6 %own.1 = (bf16[1024,2048]{1,0:T(8,128)(2,1)S(1)}, bf16[2048,1024]{1,0:T(8,128)(2,1)S(1)}, f32[2048,128]{1,0:T(8,128)S(1)}, f32[2048,128]{1,0:T(8,128)S(1)}, f32[...) custom-call(bf16[16,144,128]{2,1,0:T(8,128)(2,1)S(1)} %all-to-all-done.got_ref, bf16[8,8,16,256]{3,2,1,0:T(8,128)(2,1)S(1)} %bitcast.14, ...), custom_call_target="tpu_custom_call" | custom-call | flops 8589934592 | bytes 1048576 | tf_op jit(solution)/shard_map/own/pallas_call | solution.py:436
  31.3 0.0 collective-permute-done.1.left_ref
  31.3 5.4 %first.1 = (f32[8,128]{1,0:T(8,128)S(1)}, f32[2048,128]{1,0:T(8,128)S(1)}) custom-call(f32[2048,128]{1,0:T(8,128)S(1)} %get-tuple-element.23.pairs_ref, bf16[8,144,128]{2,1,0:T(8,128)(2,1)S(1)} %collective-permute-done.1.left_ref, bf16[8,8,16,256]{3,2,1,0:T(8,128)(2,1)S(1)} %bitcast.15, f32[128,256]{1,0:T(8,128)S(1)} %multiply_reduce_fusion.norm_ref, ...), custom_call_target="tpu_custom_call" | custom-call | flops 8589934592 | bytes 1048576 | tf_op jit(solution)/shard_map/first/pallas_call | solution.py:439
  36.7 0.0 collective-permute-done.left_ref
  36.7 5.8 %second.1 = (f32[8,128]{1,0:T(8,128)S(1)}, f32[16,128]{1,0:T(8,128)S(1)}) custom-call(f32[2048,128]{1,0:T(8,128)S(1)} %get-tuple-element.23.pairs_ref, bf16[8,144,128]{2,1,0:T(8,128)(2,1)S(1)} %collective-permute-done.left_ref, bf16[8,8,16,256]{3,2,1,0:T(8,128)(2,1)S(1)} %bitcast.16, f32[128,256]{1,0:T(8,128)S(1)} %multiply_reduce_fusion.norm_ref, ...), custom_call_target="tpu_custom_call" | custom-call | flops 8589934592 | bytes 1048576 | tf_op jit(solution)/shard_map/second/pallas_call | solution.py:442
  42.5 1.3 %collective-permute-start.2 = (f32[16,128]{1,0:T(8,128)S(1)}, f32[16,128]{1,0:T(8,128)S(1)}, u32[]{:S(2)}, u32[]{:S(2)}) collective-permute-start(f32[16,128]{1,0:T(8,128)S(1)} %pad_maximum_fusion.1), channel_id=1, source_target_pairs={{0,7},{1,0},{2,1},{3,2},{4,3},{5,4},{6,5},{7,6},{8,15},{9,8},{10,9... | collective-permute-start | bytes 24584 | tf_op jit(solution)/shard_map/ppermute | solution.py:425
  43.8 3.3 %within.1 = f32[16,128]{1,0:T(8,128)S(1)} custom-call(bf16[16,144,128]{2,1,0:T(8,128)(2,1)S(1)} %all-to-all-done.got_ref, bf16[1024,2048]{1,0:T(8,128)(2,1)S(1)} %get-tuple-element.18.ut_ref, bf16[2048,1024]{1,0:T(8,128)(2,1)S(1)} %get-tuple-element.19.u_ref, f32[2048,128]{1,0:T(8,128)S(1)} %get-tuple-element.20.slots_ref, ...), custom_call_target="tpu_custom_call" | custom-call | flops 4294967296 | bytes 1048576 | tf_op jit(solution)/shard_map/within/pallas_call | solution.py:447
  47.1 0.0 collective-permute-done.2
  47.2 11.2 %all_to_all.10.got_ref = f32[16,2,128]{2,1,0:T(2,128)S(1)} all-to-all(f32[16,2,128]{2,1,0:T(2,128)S(1)} %pad_maximum_fusion), channel_id=1, replica_groups=mesh['shard'=16,'blk'=8] {'shard'}, dimensions={0} | all-to-all | bytes 32768 | tf_op jit(solution)/shard_map/all_to_all | solution.py:469
  58.4 0.7 %pick.1 = (f32[8,128]{1,0:T(8,128)}, f32[8,128]{1,0:T(8,128)}) custom-call(f32[16,2,128]{2,1,0:T(2,128)S(1)} %all_to_all.10.got_ref, s32[8,128]{1,0:T(8,128)S(1)} %get-tuple-element.28.dest_ref, s32[8,128]{1,0:T(8,128)S(1)} %get-tuple-element.29.rank_ref), custom_call_target="tpu_custom_call" | custom-call | bytes 1048576 | tf_op jit(solution)/shard_map/pick/pallas_call | solution.py:470
  (4 shorter events, 0.1 us)
Async XLA Ops:
  4.0 19.9 %all-to-all-start = ((bf16[16,144,128]{2,1,0:T(8,128)(2,1)}), bf16[16,144,128]{2,1,0:T(8,128)(2,1)S(1)}, u32[]{:S(2)}, u32[]{:S(2)}) async-start(bf16[16,144,128]{2,1,0:T(8,128)(2,1)} %get-tuple-element.17), calls=%async_computation | async-start | bytes 1179648 | tf_op jit(solution)/shard_map/all_to_all | solution.py:462
  24.0 7.4 %collective-permute-start.1 = (bf16[8,144,128]{2,1,0:T(8,128)(2,1)S(1)}, bf16[8,144,128]{2,1,0:T(8,128)(2,1)S(1)}, u32[]{:S(2)}, u32[]{:S(2)}) collective-permute-start(bf16[8,144,128]{2,1,0:T(8,128)(2,1)S(1)} %get-tuple-element.32), channel_id=1, source_target_pairs={{0,1},{1,2},{2,3},{3,4},{4,5},{5,6},{6,7},{7,0},{8,9},{9,10},{10,1... | collective-permute-start | bytes 884744 | tf_op jit(solution)/shard_map/ppermute | solution.py:425
  24.0 12.7 %collective-permute-start = (bf16[8,144,128]{2,1,0:T(8,128)(2,1)S(1)}, bf16[8,144,128]{2,1,0:T(8,128)(2,1)S(1)}, u32[]{:S(2)}, u32[]{:S(2)}) collective-permute-start(bf16[8,144,128]{2,1,0:T(8,128)(2,1)S(1)} %get-tuple-element.33), channel_id=1, source_target_pairs={{0,1},{1,2},{2,3},{3,4},{4,5},{5,6},{6,7},{7,0},{8,9},{9,10},{10,1... | collective-permute-start | bytes 884744 | tf_op jit(solution)/shard_map/ppermute | solution.py:425
  42.5 4.6 %collective-permute-start.2 = (f32[16,128]{1,0:T(8,128)S(1)}, f32[16,128]{1,0:T(8,128)S(1)}, u32[]{:S(2)}, u32[]{:S(2)}) collective-permute-start(f32[16,128]{1,0:T(8,128)S(1)} %pad_maximum_fusion.1), channel_id=1, source_target_pairs={{0,7},{1,0},{2,1},{3,2},{4,3},{5,4},{6,5},{7,6},{8,15},{9,8},{10,9... | collective-permute-start | bytes 24584 | tf_op jit(solution)/shard_map/ppermute | solution.py:425

commit v4 on v3

--- a/solution.py
+++ b/solution.py
@@ -207,13 +207,13 @@
     return [scale_of(t) for t in totals]
 
 
-def chunk_scores(n, parts, u_ref, ut, keys_ref, line_of, best_ref, fresh, own, between):
+def chunk_scores(n, parts, u_ref, ut, keys_ref, line_of, best_ref, old_ref, own, between):
     cols = [jnp.full((8, LANES), -1.0, jnp.float32)] * PER
     for q, rows in enumerate(parts):
         scores = jnp.dot(u_ref[rows, :], ut[...], preferred_element_type=jnp.float32)
         between(q)
         key = tiles(keys_ref[rows, :])
-        best = None if fresh(rows) else tiles(best_ref[rows, :])
+        best = None if old_ref is None else tiles(old_ref[rows, :])
         for h in range(PER):
             part = tiles(scores[:, h * LANES : (h + 1) * LANES])
             ok = key == line_of(h)[None]
@@ -227,7 +227,7 @@
     return [jnp.max(c, axis=0, keepdims=True) for c in cols]
 
 
-def own_piece(n, got_ref, u_ref, ut_ref, keys_ref, best_ref, out_ref, between):
+def own_piece(n, got_ref, u_ref, ut_ref, keys_ref, best_ref, out_ref, between, alone=False):
     cols = chunk_scores(
         n,
         parts_of((n + 1) * SIDE),
@@ -236,12 +236,12 @@
         keys_ref,
         lambda h: key_line(got_ref, n * PER + h, 0),
         best_ref,
-        lambda rows: False,
+        None if alone else best_ref,
         True,
         between,
     )
     for h in range(PER):
-        j = n * PER + h
+        j = h if alone else n * PER + h
         out_ref[j : j + 1, :] = cols[h]
 
 
@@ -285,61 +285,131 @@
             turn_chunk(n)
 
 
-def within_kernel(got_ref, ut_ref, u_ref, slots_ref, best_in, out_in, out_ref, best_ref):
-    out_ref[...] = out_in[...]
-    best_ref[...] = best_in[...]
-    for n in range(EARLY, CHUNKS):
-        own_piece(n, got_ref, u_ref, ut_ref, slots_ref, best_ref, out_ref, lambda q: None)
-    for j in range(SHARDS):
+def fold_rows(best_ref, out_ref, rows, join):
+    for j in range(rows.start // LANES, rows.stop // LANES):
         row = fold_lanes(best_ref[j * LANES : (j + 1) * LANES, :])
-        out_ref[j : j + 1, :] = jnp.maximum(out_ref[j : j + 1, :], row)
-
-
-def across_kernel(pairs_ref, left_ref, table_ref, norm_ref, u_ref, *rest):
-    last = len(rest) == 5
-    if last:
-        best_in, out_ref, row_ref, ut_a, ut_b = rest
-        best_ref = best_in
-    else:
-        out_ref, best_ref, ut_a, ut_b = rest
+        if join:
+            row = jnp.maximum(out_ref[j : j + 1, :], row)
+        out_ref[j : j + 1, :] = row
+
+
+def within_kernel(
+    got_ref, ut_ref, u_ref, slots_ref, best_in, early_in, best_more, more_in, out_ref, best_ref
+):
+    out_ref[...] = early_in[...]
+    out_ref[EARLY * PER : (EARLY + 1) * PER, :] = more_in[...]
+    rows = (EARLY + 1) * SIDE
+    best_ref[:rows, :] = jnp.maximum(best_in[:rows, :], best_more[...])
+    best_ref[rows:, :] = best_in[rows:, :]
+    parts = parts_of(RECV)
+
+    def between(n, q):
+        if n == CHUNKS - 1 and q > 0:
+            fold_rows(best_ref, out_ref, parts[q - 1], True)
+
+    for n in range(EARLY + 1, CHUNKS):
+        own_piece(
+            n, got_ref, u_ref, ut_ref, slots_ref, best_ref, out_ref, lambda q: between(n, q)
+        )
+    fold_rows(best_ref, out_ref, parts[-1], True)
+
+
+def decode_left(left_ref, table_ref, j, groups, scale, ut):
+    for g in groups:
+        for h in range(PER):
+            decode_part(left_ref, table_ref, j + h, g, scale[h], ut, block_lanes(h))
+
+
+def share(groups, q, count):
+    return range(q * groups // count, (q + 1) * groups // count)
+
+
+def left_scores(left_ref, j, pairs_ref, u_ref, ut, best_ref, old_ref, out_ref, row, between):
+    cols = chunk_scores(
+        0,
+        parts_of(RECV),
+        u_ref,
+        ut,
+        pairs_ref,
+        lambda h: key_line(left_ref, j + h, 0),
+        best_ref,
+        old_ref,
+        False,
+        between,
+    )
+    for h in range(PER):
+        out_ref[row + h : row + h + 1, :] = cols[h]
+
+
+def first_kernel(
+    pairs_ref, left_ref, table_ref, norm_ref, u_ref, got_ref, own_ref, slots_ref,
+    out_ref, best_ref, ut_b, best_more, more_ref, ut_a,
+):
     uts = (ut_a, ut_b)
-    chunks = left_ref.shape[0] // PER
-    parts = parts_of(RECV)
-
-    def decode_chunk(n, groups, scale):
-        for g in groups:
-            for h in range(PER):
-                j = n * PER + h
-                decode_part(left_ref, table_ref, j, g, scale[h], uts[n % 2], block_lanes(h))
-
-    decode_chunk(0, range(GROUPS), scales(left_ref, norm_ref, 0))
-    for n in range(chunks):
-        if n + 1 < chunks:
-            scale = scales(left_ref, norm_ref, n + 1)
-
-        def between(q):
-            if n + 1 < chunks:
-                count = len(parts)
-                decode_chunk(n + 1, range(q * GROUPS // count, (q + 1) * GROUPS // count), scale)
-
-        cols = chunk_scores(
-            n,
-            parts,
+    scale = scales(left_ref, norm_ref, 0)
+    count = len(parts_of((EARLY + 1) * SIDE))
+    own_piece(
+        EARLY,
+        got_ref,
+        u_ref,
+        own_ref,
+        slots_ref,
+        best_more,
+        more_ref,
+        lambda q: decode_left(left_ref, table_ref, 0, share(GROUPS, q, count), scale, ut_a),
+        True,
+    )
+    for n in range(HALF // PER - 1):
+        j = (n + 1) * PER
+        scale = scales(left_ref, norm_ref, n + 1)
+        left_scores(
+            left_ref,
+            n * PER,
+            pairs_ref,
             u_ref,
             uts[n % 2],
+            best_ref,
+            best_ref if n else None,
+            out_ref,
+            n * PER,
+            lambda q: decode_left(
+                left_ref, table_ref, j, share(GROUPS, q, 2), scale, uts[(n + 1) % 2]
+            ),
+        )
+
+
+def second_kernel(
+    pairs_ref, before_ref, left_ref, table_ref, norm_ref, u_ref, best_in, ut_in,
+    out_ref, row_ref, ut_a, ut_b, best_ref,
+):
+    uts = (ut_in, ut_a, ut_b)
+    parts = parts_of(RECV)
+    chunks = HALF // PER
+    for n in range(chunks + 1):
+        now = uts[0] if n == 0 else uts[1 + (n - 1) % 2]
+        scale = scales(left_ref, norm_ref, n) if n < chunks else None
+
+        def between(q):
+            if n < chunks:
+                decode_left(
+                    left_ref, table_ref, n * PER, share(GROUPS, q, 2), scale, uts[1 + n % 2]
+                )
+            elif q > 0:
+                fold_rows(best_ref, row_ref, parts[q - 1], False)
+
+        left_scores(
+            left_ref if n else before_ref,
+            (n - 1) * PER if n else HALF - PER,
             pairs_ref,
-            lambda h: key_line(left_ref, n * PER + h, 0),
+            u_ref,
+            now,
             best_ref,
-            lambda rows: n == 0 and not last,
-            False,
+            best_ref if n else best_in,
+            out_ref,
+            n * PER,
             between,
         )
-        for h in range(PER):
-            j = n * PER + h
-            out_ref[j : j + 1, :] = cols[h]
-    if last:
-        for j in range(SHARDS):
-            row_ref[j : j + 1, :] = fold_lanes(best_ref[j * LANES : (j + 1) * LANES, :])
+    fold_rows(best_ref, row_ref, parts[-1], False)
 
 
 def pick_kernel(got_ref, dest_ref, rank_ref, within_ref, near_ref):
@@ -386,11 +456,28 @@
     ],
     3,
 )
-UTS = [pltpu.VMEM((EMB, SIDE), bf16)] * 2
+UT = pltpu.VMEM((EMB, SIDE), bf16)
+BEST = pltpu.VMEM((RECV, LANES), f32)
 HALF = SHARDS // 2
-K_FIRST = (across_kernel, [shape((HALF, LANES), f32), shape((RECV, LANES), f32)], 5, UTS)
-K_SECOND = (across_kernel, [shape((HALF, LANES), f32), shape((SHARDS, LANES), f32)], 6, UTS)
-K_WITHIN = (within_kernel, [shape((SHARDS, LANES), f32)], 6, [pltpu.VMEM((RECV, LANES), f32)])
+K_FIRST = (
+    first_kernel,
+    [
+        shape((HALF - PER, LANES), f32),
+        shape((RECV, LANES), f32),
+        shape((EMB, SIDE), bf16),
+        shape(((EARLY + 1) * SIDE, LANES), f32),
+        shape((PER, LANES), f32),
+    ],
+    8,
+    [UT],
+)
+K_SECOND = (
+    second_kernel,
+    [shape((HALF + PER, LANES), f32), shape((SHARDS, LANES), f32)],
+    8,
+    [UT, UT, BEST],
+)
+K_WITHIN = (within_kernel, [shape((SHARDS, LANES), f32)], 8, [BEST])
 K_PICK = (pick_kernel, [shape((8, LANES), f32), shape((8, LANES), f32)], 3)
 
 
@@ -436,16 +523,16 @@
     ut, u, slots, pairs, best, early = kernel_call(*K_OWN, name="own", flops=8 << 30)(
         got, table, norms
     )
-    cols_a, partial = kernel_call(*K_FIRST, name="first", flops=8 << 30)(
-        pairs, left[0], table, norms, u
-    )
+    cols_a, partial, ut_last, best_more, more = kernel_call(
+        *K_FIRST, name="first", flops=8 << 30
+    )(pairs, left[0], table, norms, u, got, ut, slots)
     cols_b, from_left = kernel_call(*K_SECOND, name="second", flops=8 << 30)(
-        pairs, left[1], table, norms, u, partial
+        pairs, left[0], left[1], table, norms, u, partial, ut_last
     )
 
     def within():
         return kernel_call(*K_WITHIN, name="within", flops=4 << 30)(
-            got, ut, u, slots, best, early
+            got, ut, u, slots, best, early, best_more, more
         )[0]
 
     return within, from_left, jnp.concatenate([cols_a, cols_b], axis=0)

time: 59.4 us -> 58.7 us (0.988)
  Pallas kernels: 24.2 us -> 23.5 us
    pallas_call x1, Pallas kernels: 5.8 us -> 6.67 us  [scores_of(): kernel_call(*K_SECOND, name='second', flops=8 << 30)]
    pallas_call x1, Pallas kernels: 3.32 us -> 2.53 us  [within(): kernel_call(*K_WITHIN, name='within', flops=4 << 30)]
    pallas_call x1, Pallas kernels: 5.37 us -> 4.62 us  [scores_of(): kernel_call(*K_FIRST, name='first', flops=8 << 30)]
  transfers between devices with their start and end apart: 4 -> 4, of which waited for: 1 -> 2; matrix products, arithmetic and copies ran while one was open for 4% -> 4% of each run, Pallas kernels for 24% -> 22%
where the time goes in v4:
time: 58.7 us; the launch traced here: 58.4 us
  Pallas kernels  23.5 us (40%)
  blocking collectives  11.2 us (19%)
  starting transfers between devices  10.9 us (19%)
  waiting for transfers between devices  9.45 us (16%)
  other arithmetic  1.4 us (2%)
  local copies, waits for them, and re-layouts  1.19 us (2%)
  between operations  0.72 us (1%)
    all_to_all x1, blocking collectives, on_device(): lax.all_to_all(answers, 'shard', split_axis=0, concat_axis=0, tiled=True)  11.2 us
    all_to_all x1, waiting for transfers between devices, on_device(): got = lax.all_to_all(send, 'shard', split_axis=0, concat_axis=0, tiled=True)  9.37 us
    all_to_all x1, starting transfers between devices, on_device(): got = lax.all_to_all(send, 'shard', split_axis=0, concat_axis=0, tiled=True)  7.98 us
    pallas_call x1, Pallas kernels, scores_of(): kernel_call(*K_SECOND, name='second', flops=8 << 30)  6.67 us
    pallas_call x1, Pallas kernels, scores_of(): kernel_call(*K_OWN, name='own', flops=8 << 30)(got, table, norms)  5.59 us
    pallas_call x1, Pallas kernels, scores_of(): kernel_call(*K_FIRST, name='first', flops=8 << 30)  4.62 us
    pallas_call x1, Pallas kernels, route_call(): pl.pallas_call(route_kernel, out_shape=[shape((SHARDS, BLOCK, LANES), bf1...  3.4 us
    ppermute x3, starting transfers between devices, from_behind(): return lax.ppermute(x, axis, [(i, (i + by) % peers) for i in range(peers)])  2.95 us
  transfers between devices with their start and end apart: 4, of which 2 were waited for; matrix products, arithmetic and copies ran while one was open for 4% of the time, Pallas kernels for 22%

profile of v4, /device:TPU:0, one launch (start us, length us, event | category | flops | bytes accessed | tf_op | source)
XLA Modules:
  0.0 58.4 jit_solution(13737435745664926547)
XLA Ops:
  0.6 3.4 %route.1 = (bf16[16,144,128]{2,1,0:T(8,128)(2,1)}, s32[8,128]{1,0:T(8,128)S(1)}, s32[8,128]{1,0:T(8,128)S(1)}) custom-call(s32[1024,128]{1,0:T(8,128)} %codes_hbm.1, s32[8,128]{1,0:T(8,128)} %bitcast.20, s32[8,128]{1,0:T(8,128)} %bitcast.21, s32[8,128]{1,0:T(8,128)} %bitcast.22), custom_call_target="tpu_custom_call" | custom-call | tf_op jit(solution)/shard_map/route/pallas_call | solution.py:487
  4.0 8.0 %all-to-all-start = ((bf16[16,144,128]{2,1,0:T(8,128)(2,1)}), bf16[16,144,128]{2,1,0:T(8,128)(2,1)S(1)}, u32[]{:S(2)}, u32[]{:S(2)}) async-start(bf16[16,144,128]{2,1,0:T(8,128)(2,1)} %get-tuple-element.20), calls=%async_computation | async-start | bytes 1179648 | tf_op jit(solution)/shard_map/all_to_all | solution.py:549
  12.0 1.1 %copy.9 = bf16[8,16,8,256]{3,1,2,0:T(8,128)(2,1)S(1)} copy(bf16[8,16,8,256]{3,2,1,0:T(8,128)(2,1)} %bitcast.18) | data formatting | bytes 1048576 | tf_op jit(solution)/shard_map/reshape | solution.py:519
  13.2 1.4 %multiply_reduce_fusion.norm_ref = f32[128,256]{1,0:T(8,128)S(1)} fusion(bf16[128,256,8]{1,2,0:T(8,128)(2,1)} %param.9), kind=kLoop, calls=%fused_computation | loop fusion | flops 753664 | bytes 655360 | tf_op jit(solution)/shard_map/reduce_sum | solution.py:518
  14.5 9.4 %all-to-all-done.got_ref = bf16[16,144,128]{2,1,0:T(8,128)(2,1)S(1)} async-done(((bf16[16,144,128]{2,1,0:T(8,128)(2,1)}), bf16[16,144,128]{2,1,0:T(8,128)(2,1)S(1)}, u32[]{:S(2)}, u32[]{:S(2)}) %all-to-all-start) | async-done | bytes 589856 | tf_op jit(solution)/shard_map/all_to_all | solution.py:549
  24.0 0.0 collective-permute-start
  24.0 1.7 %collective-permute-start.1 = (bf16[8,144,128]{2,1,0:T(8,128)(2,1)S(1)}, bf16[8,144,128]{2,1,0:T(8,128)(2,1)S(1)}, u32[]{:S(2)}, u32[]{:S(2)}) collective-permute-start(bf16[8,144,128]{2,1,0:T(8,128)(2,1)S(1)} %get-tuple-element.38), channel_id=1, source_target_pairs={{0,1},{1,2},{2,3},{3,4},{4,5},{5,6},{6,7},{7,0},{8,9},{9,10},{10,1... | collective-permute-start | bytes 884744 | tf_op jit(solution)/shard_map/ppermute | solution.py:512
  25.7 5.6 %own.1 = (bf16[1024,2048]{1,0:T(8,128)(2,1)S(1)}, bf16[2048,1024]{1,0:T(8,128)(2,1)S(1)}, f32[2048,128]{1,0:T(8,128)S(1)}, f32[2048,128]{1,0:T(8,128)S(1)}, f32[...) custom-call(bf16[16,144,128]{2,1,0:T(8,128)(2,1)S(1)} %all-to-all-done.got_ref, bf16[8,8,16,256]{3,2,1,0:T(8,128)(2,1)S(1)} %bitcast.14, ...), custom_call_target="tpu_custom_call" | custom-call | flops 8589934592 | bytes 1048576 | tf_op jit(solution)/shard_map/own/pallas_call | solution.py:523
  31.3 0.1 collective-permute-done.left_ref.before_ref
  31.3 4.6 %first.1 = (f32[6,128]{1,0:T(8,128)S(1)}, f32[2048,128]{1,0:T(8,128)S(1)}, bf16[1024,256]{1,0:T(8,128)(2,1)S(1)}, f32[1536,128]{1,0:T(8,128)S(1)}, f32[2,128]{1,0:T(2,128)S(1)}) custom-call(f32[2048,128]{1,0:T(8,128)S(1)} %get-tuple-element.26.pairs_ref, bf16[8,144,128]{2,1,0:T(8,128)(2,1)S(1)} %collective-permute-done.left_ref.before_ref, ...), custom_call_target="tpu_custom_call" | custom-call | flops 8589934592 | bytes 1048576 | tf_op jit(solution)/shard_map/first/pallas_call | solution.py:526
  36.0 0.0 collective-permute-done.1.left_ref
  36.0 6.7 %second.1 = (f32[10,128]{1,0:T(8,128)S(1)}, f32[16,128]{1,0:T(8,128)S(1)}) custom-call(f32[2048,128]{1,0:T(8,128)S(1)} %get-tuple-element.26.pairs_ref, bf16[8,144,128]{2,1,0:T(8,128)(2,1)S(1)} %collective-permute-done.left_ref.before_ref, bf16[8,144,128]{2,1,0:T(8,128)(2,1)S(1)} %collective-permute-done.1.left_ref, bf16[8,8,16,256]{3,2,1,0:T(8,128)(2,1)S(1)} %bitcast.16, ...), custom_call_target="tpu_custom_call" | custom-call | flops 8589934592 | bytes 1048576 | tf_op jit(solution)/shard_map/second/pallas_call | solution.py:529
  42.7 1.3 %collective-permute-start.2 = (f32[16,128]{1,0:T(8,128)S(1)}, f32[16,128]{1,0:T(8,128)S(1)}, u32[]{:S(2)}, u32[]{:S(2)}) collective-permute-start(f32[16,128]{1,0:T(8,128)S(1)} %pad_maximum_fusion.1), channel_id=1, source_target_pairs={{0,7},{1,0},{2,1},{3,2},{4,3},{5,4},{6,5},{7,6},{8,15},{9,8},{10,9... | collective-permute-start | bytes 24584 | tf_op jit(solution)/shard_map/ppermute | solution.py:512
  43.9 2.5 %within.1 = f32[16,128]{1,0:T(8,128)S(1)} custom-call(bf16[16,144,128]{2,1,0:T(8,128)(2,1)S(1)} %all-to-all-done.got_ref, bf16[1024,2048]{1,0:T(8,128)(2,1)S(1)} %get-tuple-element.21.own_ref.ut_ref, bf16[2048,1024]{1,0:T(8,128)(2,1)S(1)} %get-tuple-element.22.u_ref, f32[2048,128]{1,0:T(8,128)S(1)} %get-tuple-element.23.slots_ref, ...), custom_call_target="tpu_custom_call" | custom-call | flops 4294967296 | bytes 1048576 | tf_op jit(solution)/shard_map/within/pallas_call | solution.py:534
  46.4 0.0 collective-permute-done.2
  46.5 11.2 %all_to_all.10.got_ref = f32[16,2,128]{2,1,0:T(2,128)S(1)} all-to-all(f32[16,2,128]{2,1,0:T(2,128)S(1)} %pad_maximum_fusion), channel_id=1, replica_groups=mesh['shard'=16,'blk'=8] {'shard'}, dimensions={0} | all-to-all | bytes 32768 | tf_op jit(solution)/shard_map/all_to_all | solution.py:556
  57.7 0.7 %pick.1 = (f32[8,128]{1,0:T(8,128)}, f32[8,128]{1,0:T(8,128)}) custom-call(f32[16,2,128]{2,1,0:T(2,128)S(1)} %all_to_all.10.got_ref, s32[8,128]{1,0:T(8,128)S(1)} %get-tuple-element.34.dest_ref, s32[8,128]{1,0:T(8,128)S(1)} %get-tuple-element.35.rank_ref), custom_call_target="tpu_custom_call" | custom-call | bytes 1048576 | tf_op jit(solution)/shard_map/pick/pallas_call | solution.py:557
  (4 shorter events, 0.1 us)
Async XLA Ops:
  4.0 19.9 %all-to-all-start = ((bf16[16,144,128]{2,1,0:T(8,128)(2,1)}), bf16[16,144,128]{2,1,0:T(8,128)(2,1)S(1)}, u32[]{:S(2)}, u32[]{:S(2)}) async-start(bf16[16,144,128]{2,1,0:T(8,128)(2,1)} %get-tuple-element.20), calls=%async_computation | async-start | bytes 1179648 | tf_op jit(solution)/shard_map/all_to_all | solution.py:549
  24.0 7.4 %collective-permute-start = (bf16[8,144,128]{2,1,0:T(8,128)(2,1)S(1)}, bf16[8,144,128]{2,1,0:T(8,128)(2,1)S(1)}, u32[]{:S(2)}, u32[]{:S(2)}) collective-permute-start(bf16[8,144,128]{2,1,0:T(8,128)(2,1)S(1)} %get-tuple-element.39), channel_id=1, source_target_pairs={{0,1},{1,2},{2,3},{3,4},{4,5},{5,6},{6,7},{7,0},{8,9},{9,10},{10,1... | collective-permute-start | bytes 884744 | tf_op jit(solution)/shard_map/ppermute | solution.py:512
  24.0 12.0 %collective-permute-start.1 = (bf16[8,144,128]{2,1,0:T(8,128)(2,1)S(1)}, bf16[8,144,128]{2,1,0:T(8,128)(2,1)S(1)}, u32[]{:S(2)}, u32[]{:S(2)}) collective-permute-start(bf16[8,144,128]{2,1,0:T(8,128)(2,1)S(1)} %get-tuple-element.38), channel_id=1, source_target_pairs={{0,1},{1,2},{2,3},{3,4},{4,5},{5,6},{6,7},{7,0},{8,9},{9,10},{10,1... | collective-permute-start | bytes 884744 | tf_op jit(solution)/shard_map/ppermute | solution.py:512
  42.7 3.8 %collective-permute-start.2 = (f32[16,128]{1,0:T(8,128)S(1)}, f32[16,128]{1,0:T(8,128)S(1)}, u32[]{:S(2)}, u32[]{:S(2)}) collective-permute-start(f32[16,128]{1,0:T(8,128)S(1)} %pad_maximum_fusion.1), channel_id=1, source_target_pairs={{0,7},{1,0},{2,1},{3,2},{4,3},{5,4},{6,5},{7,6},{8,15},{9,8},{10,9... | collective-permute-start | bytes 24584 | tf_op jit(solution)/shard_map/ppermute | solution.py:512

commit v5 on v4

--- a/solution.py
+++ b/solution.py
@@ -126,6 +126,7 @@
 OWNERS = 2
 
 
+FOLD = 6
 EARLY = 5
 SIDE = 256
 PER = SIDE // CAP
@@ -294,7 +295,8 @@
 
 
 def within_kernel(
-    got_ref, ut_ref, u_ref, slots_ref, best_in, early_in, best_more, more_in, out_ref, best_ref
+    got_ref, ut_ref, u_ref, slots_ref, best_in, early_in, best_more, more_in, crossed_ref,
+    out_ref, row_ref, best_ref,
 ):
     out_ref[...] = early_in[...]
     out_ref[EARLY * PER : (EARLY + 1) * PER, :] = more_in[...]
@@ -304,6 +306,8 @@
     parts = parts_of(RECV)
 
     def between(n, q):
+        if n == FOLD:
+            fold_rows(crossed_ref, row_ref, parts[q], False)
         if n == CHUNKS - 1 and q > 0:
             fold_rows(best_ref, out_ref, parts[q - 1], True)
 
@@ -380,10 +384,9 @@
 
 def second_kernel(
     pairs_ref, before_ref, left_ref, table_ref, norm_ref, u_ref, best_in, ut_in,
-    out_ref, row_ref, ut_a, ut_b, best_ref,
+    out_ref, best_ref, ut_a, ut_b,
 ):
     uts = (ut_in, ut_a, ut_b)
-    parts = parts_of(RECV)
     chunks = HALF // PER
     for n in range(chunks + 1):
         now = uts[0] if n == 0 else uts[1 + (n - 1) % 2]
@@ -394,8 +397,6 @@
                 decode_left(
                     left_ref, table_ref, n * PER, share(GROUPS, q, 2), scale, uts[1 + n % 2]
                 )
-            elif q > 0:
-                fold_rows(best_ref, row_ref, parts[q - 1], False)
 
         left_scores(
             left_ref if n else before_ref,
@@ -409,7 +410,6 @@
             n * PER,
             between,
         )
-    fold_rows(best_ref, row_ref, parts[-1], False)
 
 
 def pick_kernel(got_ref, dest_ref, rank_ref, within_ref, near_ref):
@@ -473,11 +473,13 @@
 )
 K_SECOND = (
     second_kernel,
-    [shape((HALF + PER, LANES), f32), shape((SHARDS, LANES), f32)],
+    [shape((HALF + PER, LANES), f32), shape((RECV, LANES), f32)],
     8,
-    [UT, UT, BEST],
+    [UT, UT],
 )
-K_WITHIN = (within_kernel, [shape((SHARDS, LANES), f32)], 8, [BEST])
+K_WITHIN = (
+    within_kernel, [shape((SHARDS, LANES), f32), shape((SHARDS, LANES), f32)], 9, [BEST]
+)
 K_PICK = (pick_kernel, [shape((8, LANES), f32), shape((8, LANES), f32)], 3)
 
 
@@ -526,16 +528,16 @@
     cols_a, partial, ut_last, best_more, more = kernel_call(
         *K_FIRST, name="first", flops=8 << 30
     )(pairs, left[0], table, norms, u, got, ut, slots)
-    cols_b, from_left = kernel_call(*K_SECOND, name="second", flops=8 << 30)(
+    cols_b, crossed = kernel_call(*K_SECOND, name="second", flops=8 << 30)(
         pairs, left[0], left[1], table, norms, u, partial, ut_last
     )
 
     def within():
         return kernel_call(*K_WITHIN, name="within", flops=4 << 30)(
-            got, ut, u, slots, best, early, best_more, more
-        )[0]
-
-    return within, from_left, jnp.concatenate([cols_a, cols_b], axis=0)
+            got, ut, u, slots, best, early, best_more, more, crossed
+        )
+
+    return within, jnp.concatenate([cols_a, cols_b], axis=0)
 
 
 def on_device(codes, cluster_ids, cluster_owner, left_pair, codebook):
@@ -548,9 +550,9 @@
     table, norms = tables_of(codebook)
     got = lax.all_to_all(send, "shard", split_axis=0, concat_axis=0, tiled=True)
     left = [from_behind(got[h * HALF : (h + 1) * HALF], "blk", 1) for h in range(2)]
-    within, from_left, for_left = scores_of(got, left, table, norms)
+    within, for_left = scores_of(got, left, table, norms)
     from_right = from_behind(for_left, "blk", -1)
-    within = within()
+    within, from_left = within()
     near = jnp.maximum(from_left, from_right)
     answers = jnp.stack([within, near], axis=1)
     back = lax.all_to_all(answers, "shard", split_axis=0, concat_axis=0, tiled=True)

time: 58.7 us -> 60.3 us (1.027)
  waiting for transfers between devices: 9.45 us -> 12.6 us
  starting transfers between devices: 10.9 us -> 9.69 us
    ppermute x3, waiting for transfers between devices: 0.07 us -> 3.22 us  [from_behind(): return lax.ppermute(x, axis, [(i, (i + by) % peers) for i in range(peers)])]
    ppermute x3, starting transfers between devices: 2.95 us -> 1.72 us  [from_behind(): return lax.ppermute(x, axis, [(i, (i + by) % peers) for i in range(peers)])]
  transfers between devices with their start and end apart: 4 -> 4, of which waited for: 2 -> 2; matrix products, arithmetic and copies ran while one was open for 4% -> 4% of each run, Pallas kernels for 22% -> 21%
where the time goes in v5:
time: 60.3 us; the launch traced here: 59.9 us
  Pallas kernels  23.1 us (38%)
  waiting for transfers between devices  12.6 us (21%)
  blocking collectives  11.2 us (19%)
  starting transfers between devices  9.69 us (16%)
  other arithmetic  1.4 us (2%)
  local copies, waits for them, and re-layouts  1.19 us (2%)
  between operations  0.73 us (1%)
    all_to_all x1, blocking collectives, on_device(): lax.all_to_all(answers, 'shard', split_axis=0, concat_axis=0, tiled=True)  11.2 us
    all_to_all x1, waiting for transfers between devices, on_device(): got = lax.all_to_all(send, 'shard', split_axis=0, concat_axis=0, tiled=True)  9.37 us
    all_to_all x1, starting transfers between devices, on_device(): got = lax.all_to_all(send, 'shard', split_axis=0, concat_axis=0, tiled=True)  7.98 us
    pallas_call x1, Pallas kernels, scores_of(): kernel_call(*K_SECOND, name='second', flops=8 << 30)  6.29 us
    pallas_call x1, Pallas kernels, scores_of(): kernel_call(*K_OWN, name='own', flops=8 << 30)(got, table, norms)  5.6 us
    pallas_call x1, Pallas kernels, scores_of(): kernel_call(*K_FIRST, name='first', flops=8 << 30)  4.59 us
    pallas_call x1, Pallas kernels, route_call(): pl.pallas_call(route_kernel, out_shape=[shape((SHARDS, BLOCK, LANES), bf1...  3.4 us
    ppermute x3, waiting for transfers between devices, from_behind(): return lax.ppermute(x, axis, [(i, (i + by) % peers) for i in range(peers)])  3.22 us
  transfers between devices with their start and end apart: 4, of which 2 were waited for; matrix products, arithmetic and copies ran while one was open for 4% of the time, Pallas kernels for 21%

profile of v5, /device:TPU:0, one launch (start us, length us, event | category | flops | bytes accessed | tf_op | source)
XLA Modules:
  0.0 59.9 jit_solution(15924068649666560627)
XLA Ops:
  0.6 3.4 %route.1 = (bf16[16,144,128]{2,1,0:T(8,128)(2,1)}, s32[8,128]{1,0:T(8,128)S(1)}, s32[8,128]{1,0:T(8,128)S(1)}) custom-call(s32[1024,128]{1,0:T(8,128)} %codes_hbm.1, s32[8,128]{1,0:T(8,128)} %bitcast.20, s32[8,128]{1,0:T(8,128)} %bitcast.21, s32[8,128]{1,0:T(8,128)} %bitcast.22), custom_call_target="tpu_custom_call" | custom-call | tf_op jit(solution)/shard_map/route/pallas_call | solution.py:489
  4.0 8.0 %all-to-all-start = ((bf16[16,144,128]{2,1,0:T(8,128)(2,1)}), bf16[16,144,128]{2,1,0:T(8,128)(2,1)S(1)}, u32[]{:S(2)}, u32[]{:S(2)}) async-start(bf16[16,144,128]{2,1,0:T(8,128)(2,1)} %get-tuple-element.22), calls=%async_computation | async-start | bytes 1179648 | tf_op jit(solution)/shard_map/all_to_all | solution.py:551
  12.0 1.1 %copy.9 = bf16[8,16,8,256]{3,1,2,0:T(8,128)(2,1)S(1)} copy(bf16[8,16,8,256]{3,2,1,0:T(8,128)(2,1)} %bitcast.18) | data formatting | bytes 1048576 | tf_op jit(solution)/shard_map/reshape | solution.py:521
  13.2 1.4 %multiply_reduce_fusion.norm_ref = f32[128,256]{1,0:T(8,128)S(1)} fusion(bf16[128,256,8]{1,2,0:T(8,128)(2,1)} %param.9), kind=kLoop, calls=%fused_computation | loop fusion | flops 753664 | bytes 655360 | tf_op jit(solution)/shard_map/reduce_sum | solution.py:520
  14.6 9.4 %all-to-all-done.got_ref = bf16[16,144,128]{2,1,0:T(8,128)(2,1)S(1)} async-done(((bf16[16,144,128]{2,1,0:T(8,128)(2,1)}), bf16[16,144,128]{2,1,0:T(8,128)(2,1)S(1)}, u32[]{:S(2)}, u32[]{:S(2)}) %all-to-all-start) | async-done | bytes 589856 | tf_op jit(solution)/shard_map/all_to_all | solution.py:551
  24.0 0.0 collective-permute-start.1
  24.0 1.7 %collective-permute-start = (bf16[8,144,128]{2,1,0:T(8,128)(2,1)S(1)}, bf16[8,144,128]{2,1,0:T(8,128)(2,1)S(1)}, u32[]{:S(2)}, u32[]{:S(2)}) collective-permute-start(bf16[8,144,128]{2,1,0:T(8,128)(2,1)S(1)} %get-tuple-element.43), channel_id=1, source_target_pairs={{0,1},{1,2},{2,3},{3,4},{4,5},{5,6},{6,7},{7,0},{8,9},{9,10},{10,1... | collective-permute-start | bytes 884744 | tf_op jit(solution)/shard_map/ppermute | solution.py:514
  25.7 5.6 %own.1 = (bf16[1024,2048]{1,0:T(8,128)(2,1)S(1)}, bf16[2048,1024]{1,0:T(8,128)(2,1)S(1)}, f32[2048,128]{1,0:T(8,128)S(1)}, f32[2048,128]{1,0:T(8,128)S(1)}, f32[...) custom-call(bf16[16,144,128]{2,1,0:T(8,128)(2,1)S(1)} %all-to-all-done.got_ref, bf16[8,8,16,256]{3,2,1,0:T(8,128)(2,1)S(1)} %bitcast.14, ...), custom_call_target="tpu_custom_call" | custom-call | flops 8589934592 | bytes 1048576 | tf_op jit(solution)/shard_map/own/pallas_call | solution.py:525
  31.3 3.2 %collective-permute-done.left_ref.before_ref = bf16[8,144,128]{2,1,0:T(8,128)(2,1)S(1)} collective-permute-done((bf16[8,144,128]{2,1,0:T(8,128)(2,1)S(1)}, bf16[8,144,128]{2,1,0:T(8,128)(2,1)S(1)}, u32[]{:S(2)}, u32[]{:S(2)}) %collective-permute-start) | collective-permute-done | bytes 294944 | tf_op jit(solution)/shard_map/ppermute | solution.py:514
  34.5 4.6 %first.1 = (f32[6,128]{1,0:T(8,128)S(1)}, f32[2048,128]{1,0:T(8,128)S(1)}, bf16[1024,256]{1,0:T(8,128)(2,1)S(1)}, f32[1536,128]{1,0:T(8,128)S(1)}, f32[2,128]{1,0:T(2,128)S(1)}) custom-call(f32[2048,128]{1,0:T(8,128)S(1)} %get-tuple-element.28.pairs_ref, bf16[8,144,128]{2,1,0:T(8,128)(2,1)S(1)} %collective-permute-done.left_ref.before_ref, ...), custom_call_target="tpu_custom_call" | custom-call | flops 8589934592 | bytes 1048576 | tf_op jit(solution)/shard_map/first/pallas_call | solution.py:528
  39.1 0.0 collective-permute-done.1.left_ref
  39.1 6.3 %second.1 = (f32[10,128]{1,0:T(8,128)S(1)}, f32[2048,128]{1,0:T(8,128)S(1)}) custom-call(f32[2048,128]{1,0:T(8,128)S(1)} %get-tuple-element.28.pairs_ref, bf16[8,144,128]{2,1,0:T(8,128)(2,1)S(1)} %collective-permute-done.left_ref.before_ref, bf16[8,144,128]{2,1,0:T(8,128)(2,1)S(1)} %collective-permute-done.1.left_ref, bf16[8,8,16,256]{3,2,1,0:T(8,128)(2,1)S(1)} %bitcast.16, ...), custom_call_target="tpu_custom_call" | custom-call | flops 8589934592 | bytes 1048576 | tf_op jit(solution)/shard_map/second/pallas_call | solution.py:531
  45.4 0.0 collective-permute-start.2
  45.4 2.5 %within.1 = (f32[16,128]{1,0:T(8,128)S(1)}, f32[16,128]{1,0:T(8,128)S(1)}) custom-call(bf16[16,144,128]{2,1,0:T(8,128)(2,1)S(1)} %all-to-all-done.got_ref, bf16[1024,2048]{1,0:T(8,128)(2,1)S(1)} %get-tuple-element.23.own_ref.ut_ref, bf16[2048,1024]{1,0:T(8,128)(2,1)S(1)} %get-tuple-element.24.u_ref, f32[2048,128]{1,0:T(8,128)S(1)} %get-tuple-element.25.slots_ref, ...), custom_call_target="tpu_custom_call" | custom-call | flops 4294967296 | bytes 1048576 | tf_op jit(solution)/shard_map/within/pallas_call | solution.py:536
  48.0 0.0 collective-permute-done.2
  48.0 11.2 %all_to_all.10.got_ref = f32[16,2,128]{2,1,0:T(2,128)S(1)} all-to-all(f32[16,2,128]{2,1,0:T(2,128)S(1)} %pad_maximum_fusion), channel_id=1, replica_groups=mesh['shard'=16,'blk'=8] {'shard'}, dimensions={0} | all-to-all | bytes 32768 | tf_op jit(solution)/shard_map/all_to_all | solution.py:558
  59.2 0.7 %pick.1 = (f32[8,128]{1,0:T(8,128)}, f32[8,128]{1,0:T(8,128)}) custom-call(f32[16,2,128]{2,1,0:T(2,128)S(1)} %all_to_all.10.got_ref, s32[8,128]{1,0:T(8,128)S(1)} %get-tuple-element.38.dest_ref, s32[8,128]{1,0:T(8,128)S(1)} %get-tuple-element.39.rank_ref), custom_call_target="tpu_custom_call" | custom-call | bytes 1048576 | tf_op jit(solution)/shard_map/pick/pallas_call | solution.py:559
  (4 shorter events, 0.1 us)
Async XLA Ops:
  4.0 19.9 %all-to-all-start = ((bf16[16,144,128]{2,1,0:T(8,128)(2,1)}), bf16[16,144,128]{2,1,0:T(8,128)(2,1)S(1)}, u32[]{:S(2)}, u32[]{:S(2)}) async-start(bf16[16,144,128]{2,1,0:T(8,128)(2,1)} %get-tuple-element.22), calls=%async_computation | async-start | bytes 1179648 | tf_op jit(solution)/shard_map/all_to_all | solution.py:551
  24.0 15.1 %collective-permute-start.1 = (bf16[8,144,128]{2,1,0:T(8,128)(2,1)S(1)}, bf16[8,144,128]{2,1,0:T(8,128)(2,1)S(1)}, u32[]{:S(2)}, u32[]{:S(2)}) collective-permute-start(bf16[8,144,128]{2,1,0:T(8,128)(2,1)S(1)} %get-tuple-element.42), channel_id=1, source_target_pairs={{0,1},{1,2},{2,3},{3,4},{4,5},{5,6},{6,7},{7,0},{8,9},{9,10},{10,1... | collective-permute-start | bytes 884744 | tf_op jit(solution)/shard_map/ppermute | solution.py:514
  24.0 10.5 %collective-permute-start = (bf16[8,144,128]{2,1,0:T(8,128)(2,1)S(1)}, bf16[8,144,128]{2,1,0:T(8,128)(2,1)S(1)}, u32[]{:S(2)}, u32[]{:S(2)}) collective-permute-start(bf16[8,144,128]{2,1,0:T(8,128)(2,1)S(1)} %get-tuple-element.43), channel_id=1, source_target_pairs={{0,1},{1,2},{2,3},{3,4},{4,5},{5,6},{6,7},{7,0},{8,9},{9,10},{10,1... | collective-permute-start | bytes 884744 | tf_op jit(solution)/shard_map/ppermute | solution.py:514
  45.4 2.6 %collective-permute-start.2 = (f32[16,128]{1,0:T(8,128)S(1)}, f32[16,128]{1,0:T(8,128)S(1)}, u32[]{:S(2)}, u32[]{:S(2)}) collective-permute-start(f32[16,128]{1,0:T(8,128)S(1)} %pad_maximum_fusion.1), channel_id=1, source_target_pairs={{0,7},{1,0},{2,1},{3,2},{4,3},{5,4},{6,5},{7,6},{8,15},{9,8},{10,9... | collective-permute-start | bytes 24584 | tf_op jit(solution)/shard_map/ppermute | solution.py:514

commit v6 on v5

--- a/solution.py
+++ b/solution.py
@@ -522,7 +522,7 @@
 
 
 def scores_of(got, left, table, norms):
-    ut, u, slots, pairs, best, early = kernel_call(*K_OWN, name="own", flops=8 << 30)(
+    ut, u, slots, pairs, best, early = kernel_call(*K_OWN, name="own", flops=2 << 30)(
         got, table, norms
     )
     cols_a, partial, ut_last, best_more, more = kernel_call(

time: 60.3 us -> 58.7 us (0.973)
  waiting for transfers between devices: 12.6 us -> 10.8 us
  starting transfers between devices: 9.69 us -> 11 us
  other arithmetic: 1.4 us -> 0.35 us
    ppermute x3, waiting for transfers between devices: 3.22 us -> 0.01 us  [from_behind(): return lax.ppermute(x, axis, [(i, (i + by) % peers) for i in range(peers)])]
    all_to_all x1, waiting for transfers between devices: 9.37 us -> 10.8 us  [on_device(): got = lax.all_to_all(send, 'shard', split_axis=0, concat_axis=0, tiled=True)]
    ppermute x3, starting transfers between devices: 1.72 us -> 3 us  [from_behind(): return lax.ppermute(x, axis, [(i, (i + by) % peers) for i in range(peers)])]
    reduce_sum x1, other arithmetic: 1.37 us -> 0.32 us  [tables_of(): norms = jnp.sum(wide * wide, axis=1)]
  transfers between devices with their start and end apart: 4 -> 4, of which waited for: 2 -> 1; matrix products, arithmetic and copies ran while one was open for 4% -> 3% of each run, Pallas kernels for 21% -> 22%
where the time goes in v6:
time: 58.7 us; the launch traced here: 58.4 us
  Pallas kernels  23.2 us (40%)
  blocking collectives  11.2 us (19%)
  starting transfers between devices  11 us (19%)
  waiting for transfers between devices  10.8 us (18%)
  local copies, waits for them, and re-layouts  1.19 us (2%)
  between operations  0.75 us (1%)
    all_to_all x1, blocking collectives, on_device(): lax.all_to_all(answers, 'shard', split_axis=0, concat_axis=0, tiled=True)  11.2 us
    all_to_all x1, waiting for transfers between devices, on_device(): got = lax.all_to_all(send, 'shard', split_axis=0, concat_axis=0, tiled=True)  10.8 us
    all_to_all x1, starting transfers between devices, on_device(): got = lax.all_to_all(send, 'shard', split_axis=0, concat_axis=0, tiled=True)  7.96 us
    pallas_call x1, Pallas kernels, scores_of(): kernel_call(*K_SECOND, name='second', flops=8 << 30)  6.29 us
    pallas_call x1, Pallas kernels, scores_of(): kernel_call(*K_OWN, name='own', flops=2 << 30)(got, table, norms)  5.6 us
    pallas_call x1, Pallas kernels, scores_of(): kernel_call(*K_FIRST, name='first', flops=8 << 30)  4.59 us
    pallas_call x1, Pallas kernels, route_call(): pl.pallas_call(route_kernel, out_shape=[shape((SHARDS, BLOCK, LANES), bf1...  3.47 us
    ppermute x3, starting transfers between devices, from_behind(): return lax.ppermute(x, axis, [(i, (i + by) % peers) for i in range(peers)])  3 us
  transfers between devices with their start and end apart: 4, of which 1 were waited for; matrix products, arithmetic and copies ran while one was open for 3% of the time, Pallas kernels for 22%

profile of v6, /device:TPU:0, one launch (start us, length us, event | category | flops | bytes accessed | tf_op | source)
XLA Modules:
  0.0 58.4 jit_solution(11937715426532327229)
XLA Ops:
  0.6 0.0 copy-start
  0.6 3.5 %route.1 = (bf16[16,144,128]{2,1,0:T(8,128)(2,1)}, s32[8,128]{1,0:T(8,128)S(1)}, s32[8,128]{1,0:T(8,128)S(1)}) custom-call(s32[1024,128]{1,0:T(8,128)} %codes_hbm.1, s32[8,128]{1,0:T(8,128)} %bitcast.20, s32[8,128]{1,0:T(8,128)} %bitcast.21, s32[8,128]{1,0:T(8,128)} %bitcast.22), custom_call_target="tpu_custom_call" | custom-call | tf_op jit(solution)/shard_map/route/pallas_call | solution.py:489
  4.1 8.0 %all-to-all-start = ((bf16[16,144,128]{2,1,0:T(8,128)(2,1)}), bf16[16,144,128]{2,1,0:T(8,128)(2,1)S(1)}, u32[]{:S(2)}, u32[]{:S(2)}) async-start(bf16[16,144,128]{2,1,0:T(8,128)(2,1)} %get-tuple-element.22), calls=%async_computation | async-start | bytes 1179648 | tf_op jit(solution)/shard_map/all_to_all | solution.py:551
  12.1 1.1 %copy.9 = bf16[8,16,8,256]{3,1,2,0:T(8,128)(2,1)S(1)} copy(bf16[8,16,8,256]{3,2,1,0:T(8,128)(2,1)} %bitcast.18) | data formatting | bytes 1048576 | tf_op jit(solution)/shard_map/reshape | solution.py:521
  13.2 10.8 %all-to-all-done.got_ref = bf16[16,144,128]{2,1,0:T(8,128)(2,1)S(1)} async-done(((bf16[16,144,128]{2,1,0:T(8,128)(2,1)}), bf16[16,144,128]{2,1,0:T(8,128)(2,1)S(1)}, u32[]{:S(2)}, u32[]{:S(2)}) %all-to-all-start) | async-done | bytes 589856 | tf_op jit(solution)/shard_map/all_to_all | solution.py:551
  24.0 0.0 collective-permute-start
  24.1 0.0 copy-done
  24.1 0.3 multiply_reduce_fusion.norm_ref
  24.4 1.7 %collective-permute-start.1 = (bf16[8,144,128]{2,1,0:T(8,128)(2,1)S(1)}, bf16[8,144,128]{2,1,0:T(8,128)(2,1)S(1)}, u32[]{:S(2)}, u32[]{:S(2)}) collective-permute-start(bf16[8,144,128]{2,1,0:T(8,128)(2,1)S(1)} %get-tuple-element.42), channel_id=1, source_target_pairs={{0,1},{1,2},{2,3},{3,4},{4,5},{5,6},{6,7},{7,0},{8,9},{9,10},{10,1... | collective-permute-start | bytes 884744 | tf_op jit(solution)/shard_map/ppermute | solution.py:514
  26.1 5.6 %own.1 = (bf16[1024,2048]{1,0:T(8,128)(2,1)S(1)}, bf16[2048,1024]{1,0:T(8,128)(2,1)S(1)}, f32[2048,128]{1,0:T(8,128)S(1)}, f32[2048,128]{1,0:T(8,128)S(1)}, f32[...) custom-call(bf16[16,144,128]{2,1,0:T(8,128)(2,1)S(1)} %all-to-all-done.got_ref, bf16[8,8,16,256]{3,2,1,0:T(8,128)(2,1)S(1)} %bitcast.14, ...), custom_call_target="tpu_custom_call" | custom-call | flops 2147483648 | bytes 1048576 | tf_op jit(solution)/shard_map/own/pallas_call | solution.py:525
  31.7 0.0 collective-permute-done.left_ref.before_ref
  31.7 4.6 %first.1 = (f32[6,128]{1,0:T(8,128)S(1)}, f32[2048,128]{1,0:T(8,128)S(1)}, bf16[1024,256]{1,0:T(8,128)(2,1)S(1)}, f32[1536,128]{1,0:T(8,128)S(1)}, f32[2,128]{1,0:T(2,128)S(1)}) custom-call(f32[2048,128]{1,0:T(8,128)S(1)} %get-tuple-element.28.pairs_ref, bf16[8,144,128]{2,1,0:T(8,128)(2,1)S(1)} %collective-permute-done.left_ref.before_ref, ...), custom_call_target="tpu_custom_call" | custom-call | flops 8589934592 | bytes 1048576 | tf_op jit(solution)/shard_map/first/pallas_call | solution.py:528
  36.3 0.0 collective-permute-done.1.left_ref
  36.3 6.3 %second.1 = (f32[10,128]{1,0:T(8,128)S(1)}, f32[2048,128]{1,0:T(8,128)S(1)}) custom-call(f32[2048,128]{1,0:T(8,128)S(1)} %get-tuple-element.28.pairs_ref, bf16[8,144,128]{2,1,0:T(8,128)(2,1)S(1)} %collective-permute-done.left_ref.before_ref, bf16[8,144,128]{2,1,0:T(8,128)(2,1)S(1)} %collective-permute-done.1.left_ref, bf16[8,8,16,256]{3,2,1,0:T(8,128)(2,1)S(1)} %bitcast.16, ...), custom_call_target="tpu_custom_call" | custom-call | flops 8589934592 | bytes 1048576 | tf_op jit(solution)/shard_map/second/pallas_call | solution.py:531
  42.6 1.3 %collective-permute-start.2 = (f32[16,128]{1,0:T(8,128)S(1)}, f32[16,128]{1,0:T(8,128)S(1)}, u32[]{:S(2)}, u32[]{:S(2)}) collective-permute-start(f32[16,128]{1,0:T(8,128)S(1)} %pad_maximum_fusion.1), channel_id=1, source_target_pairs={{0,7},{1,0},{2,1},{3,2},{4,3},{5,4},{6,5},{7,6},{8,15},{9,8},{10,9... | collective-permute-start | bytes 24584 | tf_op jit(solution)/shard_map/ppermute | solution.py:514
  43.9 2.5 %within.1 = (f32[16,128]{1,0:T(8,128)S(1)}, f32[16,128]{1,0:T(8,128)S(1)}) custom-call(bf16[16,144,128]{2,1,0:T(8,128)(2,1)S(1)} %all-to-all-done.got_ref, bf16[1024,2048]{1,0:T(8,128)(2,1)S(1)} %get-tuple-element.23.own_ref.ut_ref, bf16[2048,1024]{1,0:T(8,128)(2,1)S(1)} %get-tuple-element.24.u_ref, f32[2048,128]{1,0:T(8,128)S(1)} %get-tuple-element.25.slots_ref, ...), custom_call_target="tpu_custom_call" | custom-call | flops 4294967296 | bytes 1048576 | tf_op jit(solution)/shard_map/within/pallas_call | solution.py:536
  46.4 0.0 collective-permute-done.2
  46.5 11.2 %all_to_all.10.got_ref = f32[16,2,128]{2,1,0:T(2,128)S(1)} all-to-all(f32[16,2,128]{2,1,0:T(2,128)S(1)} %pad_maximum_fusion), channel_id=1, replica_groups=mesh['shard'=16,'blk'=8] {'shard'}, dimensions={0} | all-to-all | bytes 32768 | tf_op jit(solution)/shard_map/all_to_all | solution.py:558
  57.7 0.7 %pick.1 = (f32[8,128]{1,0:T(8,128)}, f32[8,128]{1,0:T(8,128)}) custom-call(f32[16,2,128]{2,1,0:T(2,128)S(1)} %all_to_all.10.got_ref, s32[8,128]{1,0:T(8,128)S(1)} %get-tuple-element.38.dest_ref, s32[8,128]{1,0:T(8,128)S(1)} %get-tuple-element.39.rank_ref), custom_call_target="tpu_custom_call" | custom-call | bytes 1048576 | tf_op jit(solution)/shard_map/pick/pallas_call | solution.py:559
  (4 shorter events, 0.1 us)
Async XLA Ops:
  0.6 23.4 %copy-start = (bf16[128,256,8]{1,2,0:T(8,128)(2,1)S(1)}, bf16[128,256,8]{1,2,0:T(8,128)(2,1)}, u32[]{:S(2)}) copy-start(bf16[128,256,8]{1,2,0:T(8,128)(2,1)} %param.9) | copy-start | bytes 1572868
  4.1 19.9 %all-to-all-start = ((bf16[16,144,128]{2,1,0:T(8,128)(2,1)}), bf16[16,144,128]{2,1,0:T(8,128)(2,1)S(1)}, u32[]{:S(2)}, u32[]{:S(2)}) async-start(bf16[16,144,128]{2,1,0:T(8,128)(2,1)} %get-tuple-element.22), calls=%async_computation | async-start | bytes 1179648 | tf_op jit(solution)/shard_map/all_to_all | solution.py:551
  24.0 7.7 %collective-permute-start = (bf16[8,144,128]{2,1,0:T(8,128)(2,1)S(1)}, bf16[8,144,128]{2,1,0:T(8,128)(2,1)S(1)}, u32[]{:S(2)}, u32[]{:S(2)}) collective-permute-start(bf16[8,144,128]{2,1,0:T(8,128)(2,1)S(1)} %get-tuple-element.43), channel_id=1, source_target_pairs={{0,1},{1,2},{2,3},{3,4},{4,5},{5,6},{6,7},{7,0},{8,9},{9,10},{10,1... | collective-permute-start | bytes 884744 | tf_op jit(solution)/shard_map/ppermute | solution.py:514
  24.4 11.9 %collective-permute-start.1 = (bf16[8,144,128]{2,1,0:T(8,128)(2,1)S(1)}, bf16[8,144,128]{2,1,0:T(8,128)(2,1)S(1)}, u32[]{:S(2)}, u32[]{:S(2)}) collective-permute-start(bf16[8,144,128]{2,1,0:T(8,128)(2,1)S(1)} %get-tuple-element.42), channel_id=1, source_target_pairs={{0,1},{1,2},{2,3},{3,4},{4,5},{5,6},{6,7},{7,0},{8,9},{9,10},{10,1... | collective-permute-start | bytes 884744 | tf_op jit(solution)/shard_map/ppermute | solution.py:514
  42.6 3.8 %collective-permute-start.2 = (f32[16,128]{1,0:T(8,128)S(1)}, f32[16,128]{1,0:T(8,128)S(1)}, u32[]{:S(2)}, u32[]{:S(2)}) collective-permute-start(f32[16,128]{1,0:T(8,128)S(1)} %pad_maximum_fusion.1), channel_id=1, source_target_pairs={{0,7},{1,0},{2,1},{3,2},{4,3},{5,4},{6,5},{7,6},{8,15},{9,8},{10,9... | collective-permute-start | bytes 24584 | tf_op jit(solution)/shard_map/ppermute | solution.py:514

commit v7 on v6

--- a/solution.py
+++ b/solution.py
@@ -549,6 +549,7 @@
     )
     table, norms = tables_of(codebook)
     got = lax.all_to_all(send, "shard", split_axis=0, concat_axis=0, tiled=True)
+    got, table, norms = lax.optimization_barrier((got, table, norms))
     left = [from_behind(got[h * HALF : (h + 1) * HALF], "blk", 1) for h in range(2)]
     within, for_left = scores_of(got, left, table, norms)
     from_right = from_behind(for_left, "blk", -1)

time: 58.7 us -> 58.4 us (level)
  waiting for transfers between devices: 10.8 us -> 9.44 us
  other arithmetic: 0.35 us -> 1.4 us
    all_to_all x1, waiting for transfers between devices: 10.8 us -> 9.37 us  [on_device(): got = lax.all_to_all(send, 'shard', split_axis=0, concat_axis=0, tiled=True)]
    reduce_sum x1, other arithmetic: 0.32 us -> 1.37 us  [tables_of(): norms = jnp.sum(wide * wide, axis=1)]
  transfers between devices with their start and end apart: 4 -> 4, of which waited for: 1 -> 2; matrix products, arithmetic and copies ran while one was open for 3% -> 4% of each run, Pallas kernels for 22% -> 22%
where the time goes in v7:
time: 58.4 us; the launch traced here: 58 us
  Pallas kernels  23.1 us (40%)
  blocking collectives  11.2 us (19%)
  starting transfers between devices  10.9 us (19%)
  waiting for transfers between devices  9.44 us (16%)
  other arithmetic  1.4 us (2%)
  local copies, waits for them, and re-layouts  1.19 us (2%)
  between operations  0.72 us (1%)
    all_to_all x1, blocking collectives, on_device(): lax.all_to_all(answers, 'shard', split_axis=0, concat_axis=0, tiled=True)  11.2 us
    all_to_all x1, waiting for transfers between devices, on_device(): got = lax.all_to_all(send, 'shard', split_axis=0, concat_axis=0, tiled=True)  9.37 us
    all_to_all x1, starting transfers between devices, on_device(): got = lax.all_to_all(send, 'shard', split_axis=0, concat_axis=0, tiled=True)  7.98 us
    pallas_call x1, Pallas kernels, scores_of(): kernel_call(*K_SECOND, name='second', flops=8 << 30)  6.3 us
    pallas_call x1, Pallas kernels, scores_of(): kernel_call(*K_OWN, name='own', flops=2 << 30)(got, table, norms)  5.6 us
    pallas_call x1, Pallas kernels, scores_of(): kernel_call(*K_FIRST, name='first', flops=8 << 30)  4.59 us
    pallas_call x1, Pallas kernels, route_call(): pl.pallas_call(route_kernel, out_shape=[shape((SHARDS, BLOCK, LANES), bf1...  3.4 us
    ppermute x3, starting transfers between devices, from_behind(): return lax.ppermute(x, axis, [(i, (i + by) % peers) for i in range(peers)])  2.96 us
  transfers between devices with their start and end apart: 4, of which 2 were waited for; matrix products, arithmetic and copies ran while one was open for 4% of the time, Pallas kernels for 22%

profile of v7, /device:TPU:0, one launch (start us, length us, event | category | flops | bytes accessed | tf_op | source)
XLA Modules:
  0.0 58.0 jit_solution(17167827831725810713)
XLA Ops:
  0.6 3.4 %route.1 = (bf16[16,144,128]{2,1,0:T(8,128)(2,1)}, s32[8,128]{1,0:T(8,128)S(1)}, s32[8,128]{1,0:T(8,128)S(1)}) custom-call(s32[1024,128]{1,0:T(8,128)} %codes_hbm.1, s32[8,128]{1,0:T(8,128)} %bitcast.20, s32[8,128]{1,0:T(8,128)} %bitcast.21, s32[8,128]{1,0:T(8,128)} %bitcast.22), custom_call_target="tpu_custom_call" | custom-call | tf_op jit(solution)/shard_map/route/pallas_call | solution.py:489
  4.0 8.0 %all-to-all-start = ((bf16[16,144,128]{2,1,0:T(8,128)(2,1)}), bf16[16,144,128]{2,1,0:T(8,128)(2,1)S(1)}, u32[]{:S(2)}, u32[]{:S(2)}) async-start(bf16[16,144,128]{2,1,0:T(8,128)(2,1)} %get-tuple-element.25), calls=%async_computation | async-start | bytes 1179648 | tf_op jit(solution)/shard_map/all_to_all | solution.py:551
  12.0 1.1 %copy.9 = bf16[8,16,8,256]{3,1,2,0:T(8,128)(2,1)S(1)} copy(bf16[8,16,8,256]{3,2,1,0:T(8,128)(2,1)} %bitcast.18) | data formatting | bytes 1048576 | tf_op jit(solution)/shard_map/reshape | solution.py:521
  13.2 1.4 %multiply_reduce_fusion.norm_ref = f32[128,256]{1,0:T(8,128)S(1)} fusion(bf16[128,256,8]{1,2,0:T(8,128)(2,1)} %param.9), kind=kLoop, calls=%fused_computation | loop fusion | flops 753664 | bytes 655360 | tf_op jit(solution)/shard_map/reduce_sum | solution.py:520
  14.6 9.4 %all-to-all-done.got_ref = bf16[16,144,128]{2,1,0:T(8,128)(2,1)S(1)} async-done(((bf16[16,144,128]{2,1,0:T(8,128)(2,1)}), bf16[16,144,128]{2,1,0:T(8,128)(2,1)S(1)}, u32[]{:S(2)}, u32[]{:S(2)}) %all-to-all-start) | async-done | bytes 589856 | tf_op jit(solution)/shard_map/all_to_all | solution.py:551
  24.0 0.0 collective-permute-start
  24.0 1.7 %collective-permute-start.1 = (bf16[8,144,128]{2,1,0:T(8,128)(2,1)S(1)}, bf16[8,144,128]{2,1,0:T(8,128)(2,1)S(1)}, u32[]{:S(2)}, u32[]{:S(2)}) collective-permute-start(bf16[8,144,128]{2,1,0:T(8,128)(2,1)S(1)} %get-tuple-element.48), channel_id=1, source_target_pairs={{0,1},{1,2},{2,3},{3,4},{4,5},{5,6},{6,7},{7,0},{8,9},{9,10},{10,1... | collective-permute-start | bytes 884744 | tf_op jit(solution)/shard_map/ppermute | solution.py:514
  25.7 5.6 %own.1 = (bf16[1024,2048]{1,0:T(8,128)(2,1)S(1)}, bf16[2048,1024]{1,0:T(8,128)(2,1)S(1)}, f32[2048,128]{1,0:T(8,128)S(1)}, f32[2048,128]{1,0:T(8,128)S(1)}, f32[...) custom-call(bf16[16,144,128]{2,1,0:T(8,128)(2,1)S(1)} %all-to-all-done.got_ref, bf16[8,8,16,256]{3,2,1,0:T(8,128)(2,1)S(1)} %bitcast.14, ...), custom_call_target="tpu_custom_call" | custom-call | flops 2147483648 | bytes 1048576 | tf_op jit(solution)/shard_map/own/pallas_call | solution.py:525
  31.3 0.1 collective-permute-done.left_ref.before_ref
  31.3 4.6 %first.1 = (f32[6,128]{1,0:T(8,128)S(1)}, f32[2048,128]{1,0:T(8,128)S(1)}, bf16[1024,256]{1,0:T(8,128)(2,1)S(1)}, f32[1536,128]{1,0:T(8,128)S(1)}, f32[2,128]{1,0:T(2,128)S(1)}) custom-call(f32[2048,128]{1,0:T(8,128)S(1)} %get-tuple-element.34.pairs_ref, bf16[8,144,128]{2,1,0:T(8,128)(2,1)S(1)} %collective-permute-done.left_ref.before_ref, ...), custom_call_target="tpu_custom_call" | custom-call | flops 8589934592 | bytes 1048576 | tf_op jit(solution)/shard_map/first/pallas_call | solution.py:528
  35.9 0.0 collective-permute-done.1.left_ref
  35.9 6.3 %second.1 = (f32[10,128]{1,0:T(8,128)S(1)}, f32[2048,128]{1,0:T(8,128)S(1)}) custom-call(f32[2048,128]{1,0:T(8,128)S(1)} %get-tuple-element.34.pairs_ref, bf16[8,144,128]{2,1,0:T(8,128)(2,1)S(1)} %collective-permute-done.left_ref.before_ref, bf16[8,144,128]{2,1,0:T(8,128)(2,1)S(1)} %collective-permute-done.1.left_ref, bf16[8,8,16,256]{3,2,1,0:T(8,128)(2,1)S(1)} %bitcast.16, ...), custom_call_target="tpu_custom_call" | custom-call | flops 8589934592 | bytes 1048576 | tf_op jit(solution)/shard_map/second/pallas_call | solution.py:531
  42.3 1.3 %collective-permute-start.2 = (f32[16,128]{1,0:T(8,128)S(1)}, f32[16,128]{1,0:T(8,128)S(1)}, u32[]{:S(2)}, u32[]{:S(2)}) collective-permute-start(f32[16,128]{1,0:T(8,128)S(1)} %pad_maximum_fusion.1), channel_id=1, source_target_pairs={{0,7},{1,0},{2,1},{3,2},{4,3},{5,4},{6,5},{7,6},{8,15},{9,8},{10,9... | collective-permute-start | bytes 24584 | tf_op jit(solution)/shard_map/ppermute | solution.py:514
  43.5 2.5 %within.1 = (f32[16,128]{1,0:T(8,128)S(1)}, f32[16,128]{1,0:T(8,128)S(1)}) custom-call(bf16[16,144,128]{2,1,0:T(8,128)(2,1)S(1)} %all-to-all-done.got_ref, bf16[1024,2048]{1,0:T(8,128)(2,1)S(1)} %get-tuple-element.29.own_ref.ut_ref, bf16[2048,1024]{1,0:T(8,128)(2,1)S(1)} %get-tuple-element.30.u_ref, f32[2048,128]{1,0:T(8,128)S(1)} %get-tuple-element.31.slots_ref, ...), custom_call_target="tpu_custom_call" | custom-call | flops 4294967296 | bytes 1048576 | tf_op jit(solution)/shard_map/within/pallas_call | solution.py:536
  46.0 0.0 collective-permute-done.2
  46.1 11.2 %all_to_all.10.got_ref = f32[16,2,128]{2,1,0:T(2,128)S(1)} all-to-all(f32[16,2,128]{2,1,0:T(2,128)S(1)} %pad_maximum_fusion), channel_id=1, replica_groups=mesh['shard'=16,'blk'=8] {'shard'}, dimensions={0} | all-to-all | bytes 32768 | tf_op jit(solution)/shard_map/all_to_all | solution.py:559
  57.3 0.7 %pick.1 = (f32[8,128]{1,0:T(8,128)}, f32[8,128]{1,0:T(8,128)}) custom-call(f32[16,2,128]{2,1,0:T(2,128)S(1)} %all_to_all.10.got_ref, s32[8,128]{1,0:T(8,128)S(1)} %get-tuple-element.44.dest_ref, s32[8,128]{1,0:T(8,128)S(1)} %get-tuple-element.45.rank_ref), custom_call_target="tpu_custom_call" | custom-call | bytes 1048576 | tf_op jit(solution)/shard_map/pick/pallas_call | solution.py:560
  (4 shorter events, 0.1 us)
Async XLA Ops:
  4.0 19.9 %all-to-all-start = ((bf16[16,144,128]{2,1,0:T(8,128)(2,1)}), bf16[16,144,128]{2,1,0:T(8,128)(2,1)S(1)}, u32[]{:S(2)}, u32[]{:S(2)}) async-start(bf16[16,144,128]{2,1,0:T(8,128)(2,1)} %get-tuple-element.25), calls=%async_computation | async-start | bytes 1179648 | tf_op jit(solution)/shard_map/all_to_all | solution.py:551
  24.0 7.4 %collective-permute-start = (bf16[8,144,128]{2,1,0:T(8,128)(2,1)S(1)}, bf16[8,144,128]{2,1,0:T(8,128)(2,1)S(1)}, u32[]{:S(2)}, u32[]{:S(2)}) collective-permute-start(bf16[8,144,128]{2,1,0:T(8,128)(2,1)S(1)} %get-tuple-element.49), channel_id=1, source_target_pairs={{0,1},{1,2},{2,3},{3,4},{4,5},{5,6},{6,7},{7,0},{8,9},{9,10},{10,1... | collective-permute-start | bytes 884744 | tf_op jit(solution)/shard_map/ppermute | solution.py:514
  24.0 11.9 %collective-permute-start.1 = (bf16[8,144,128]{2,1,0:T(8,128)(2,1)S(1)}, bf16[8,144,128]{2,1,0:T(8,128)(2,1)S(1)}, u32[]{:S(2)}, u32[]{:S(2)}) collective-permute-start(bf16[8,144,128]{2,1,0:T(8,128)(2,1)S(1)} %get-tuple-element.48), channel_id=1, source_target_pairs={{0,1},{1,2},{2,3},{3,4},{4,5},{5,6},{6,7},{7,0},{8,9},{9,10},{10,1... | collective-permute-start | bytes 884744 | tf_op jit(solution)/shard_map/ppermute | solution.py:514
  42.3 3.8 %collective-permute-start.2 = (f32[16,128]{1,0:T(8,128)S(1)}, f32[16,128]{1,0:T(8,128)S(1)}, u32[]{:S(2)}, u32[]{:S(2)}) collective-permute-start(f32[16,128]{1,0:T(8,128)S(1)} %pad_maximum_fusion.1), channel_id=1, source_target_pairs={{0,7},{1,0},{2,1},{3,2},{4,3},{5,4},{6,5},{7,6},{8,15},{9,8},{10,9... | collective-permute-start | bytes 24584 | tf_op jit(solution)/shard_map/ppermute | solution.py:514

commit v8 on v7

--- a/solution.py
+++ b/solution.py
@@ -127,7 +127,7 @@
 
 
 FOLD = 6
-EARLY = 5
+EARLY = 4
 SIDE = 256
 PER = SIDE // CAP
 CHUNKS = RECV // SIDE
@@ -522,7 +522,7 @@
 
 
 def scores_of(got, left, table, norms):
-    ut, u, slots, pairs, best, early = kernel_call(*K_OWN, name="own", flops=2 << 30)(
+    ut, u, slots, pairs, best, early = kernel_call(*K_OWN, name="own", flops=1 << 30)(
         got, table, norms
     )
     cols_a, partial, ut_last, best_more, more = kernel_call(

time: 58.4 us -> 59 us (1.010)
  Pallas kernels: 23.1 us -> 23.8 us
    pallas_call x1, Pallas kernels: 2.53 us -> 3.35 us  [within(): kernel_call(*K_WITHIN, name='within', flops=4 << 30)]
  transfers between devices with their start and end apart: 4 -> 4, of which waited for: 2 -> 2; matrix products, arithmetic and copies ran while one was open for 4% -> 4% of each run, Pallas kernels for 22% -> 23%
where the time goes in v8:
time: 59 us; the launch traced here: 58.7 us
  Pallas kernels  23.8 us (40%)
  blocking collectives  11.2 us (19%)
  starting transfers between devices  10.9 us (18%)
  waiting for transfers between devices  9.47 us (16%)
  other arithmetic  1.4 us (2%)
  local copies, waits for them, and re-layouts  1.19 us (2%)
  between operations  0.72 us (1%)
    all_to_all x1, blocking collectives, on_device(): lax.all_to_all(answers, 'shard', split_axis=0, concat_axis=0, tiled=True)  11.2 us
    all_to_all x1, waiting for transfers between devices, on_device(): got = lax.all_to_all(send, 'shard', split_axis=0, concat_axis=0, tiled=True)  9.37 us
    all_to_all x1, starting transfers between devices, on_device(): got = lax.all_to_all(send, 'shard', split_axis=0, concat_axis=0, tiled=True)  7.98 us
    pallas_call x1, Pallas kernels, scores_of(): kernel_call(*K_SECOND, name='second', flops=8 << 30)  6.3 us
    pallas_call x1, Pallas kernels, scores_of(): kernel_call(*K_OWN, name='own', flops=1 << 30)(got, table, norms)  5.57 us
    pallas_call x1, Pallas kernels, scores_of(): kernel_call(*K_FIRST, name='first', flops=8 << 30)  4.48 us
    pallas_call x1, Pallas kernels, route_call(): pl.pallas_call(route_kernel, out_shape=[shape((SHARDS, BLOCK, LANES), bf1...  3.4 us
    pallas_call x1, Pallas kernels, within(): kernel_call(*K_WITHIN, name='within', flops=4 << 30)  3.35 us
  transfers between devices with their start and end apart: 4, of which 2 were waited for; matrix products, arithmetic and copies ran while one was open for 4% of the time, Pallas kernels for 23%

profile of v8, /device:TPU:0, one launch (start us, length us, event | category | flops | bytes accessed | tf_op | source)
XLA Modules:
  0.0 58.7 jit_solution(3635668007278992336)
XLA Ops:
  0.6 3.4 %route.1 = (bf16[16,144,128]{2,1,0:T(8,128)(2,1)}, s32[8,128]{1,0:T(8,128)S(1)}, s32[8,128]{1,0:T(8,128)S(1)}) custom-call(s32[1024,128]{1,0:T(8,128)} %codes_hbm.1, s32[8,128]{1,0:T(8,128)} %bitcast.20, s32[8,128]{1,0:T(8,128)} %bitcast.21, s32[8,128]{1,0:T(8,128)} %bitcast.22), custom_call_target="tpu_custom_call" | custom-call | tf_op jit(solution)/shard_map/route/pallas_call | solution.py:489
  4.0 8.0 %all-to-all-start = ((bf16[16,144,128]{2,1,0:T(8,128)(2,1)}), bf16[16,144,128]{2,1,0:T(8,128)(2,1)S(1)}, u32[]{:S(2)}, u32[]{:S(2)}) async-start(bf16[16,144,128]{2,1,0:T(8,128)(2,1)} %get-tuple-element.25), calls=%async_computation | async-start | bytes 1179648 | tf_op jit(solution)/shard_map/all_to_all | solution.py:551
  12.0 1.1 %copy.9 = bf16[8,16,8,256]{3,1,2,0:T(8,128)(2,1)S(1)} copy(bf16[8,16,8,256]{3,2,1,0:T(8,128)(2,1)} %bitcast.18) | data formatting | bytes 1048576 | tf_op jit(solution)/shard_map/reshape | solution.py:521
  13.2 1.4 %multiply_reduce_fusion.norm_ref = f32[128,256]{1,0:T(8,128)S(1)} fusion(bf16[128,256,8]{1,2,0:T(8,128)(2,1)} %param.9), kind=kLoop, calls=%fused_computation | loop fusion | flops 753664 | bytes 655360 | tf_op jit(solution)/shard_map/reduce_sum | solution.py:520
  14.6 9.4 %all-to-all-done.got_ref = bf16[16,144,128]{2,1,0:T(8,128)(2,1)S(1)} async-done(((bf16[16,144,128]{2,1,0:T(8,128)(2,1)}), bf16[16,144,128]{2,1,0:T(8,128)(2,1)S(1)}, u32[]{:S(2)}, u32[]{:S(2)}) %all-to-all-start) | async-done | bytes 589856 | tf_op jit(solution)/shard_map/all_to_all | solution.py:551
  24.0 0.0 collective-permute-start
  24.0 1.7 %collective-permute-start.1 = (bf16[8,144,128]{2,1,0:T(8,128)(2,1)S(1)}, bf16[8,144,128]{2,1,0:T(8,128)(2,1)S(1)}, u32[]{:S(2)}, u32[]{:S(2)}) collective-permute-start(bf16[8,144,128]{2,1,0:T(8,128)(2,1)S(1)} %get-tuple-element.48), channel_id=1, source_target_pairs={{0,1},{1,2},{2,3},{3,4},{4,5},{5,6},{6,7},{7,0},{8,9},{9,10},{10,1... | collective-permute-start | bytes 884744 | tf_op jit(solution)/shard_map/ppermute | solution.py:514
  25.7 5.6 %own.1 = (bf16[1024,2048]{1,0:T(8,128)(2,1)S(1)}, bf16[2048,1024]{1,0:T(8,128)(2,1)S(1)}, f32[2048,128]{1,0:T(8,128)S(1)}, f32[2048,128]{1,0:T(8,128)S(1)}, f32[...) custom-call(bf16[16,144,128]{2,1,0:T(8,128)(2,1)S(1)} %all-to-all-done.got_ref, bf16[8,8,16,256]{3,2,1,0:T(8,128)(2,1)S(1)} %bitcast.14, ...), custom_call_target="tpu_custom_call" | custom-call | flops 1073741824 | bytes 1048576 | tf_op jit(solution)/shard_map/own/pallas_call | solution.py:525
  31.3 0.1 collective-permute-done.left_ref.before_ref
  31.3 4.5 %first.1 = (f32[6,128]{1,0:T(8,128)S(1)}, f32[2048,128]{1,0:T(8,128)S(1)}, bf16[1024,256]{1,0:T(8,128)(2,1)S(1)}, f32[1280,128]{1,0:T(8,128)S(1)}, f32[2,128]{1,0:T(2,128)S(1)}) custom-call(f32[2048,128]{1,0:T(8,128)S(1)} %get-tuple-element.34.pairs_ref, bf16[8,144,128]{2,1,0:T(8,128)(2,1)S(1)} %collective-permute-done.left_ref.before_ref, ...), custom_call_target="tpu_custom_call" | custom-call | flops 8589934592 | bytes 1048576 | tf_op jit(solution)/shard_map/first/pallas_call | solution.py:528
  35.8 0.0 collective-permute-done.1.left_ref
  35.8 6.3 %second.1 = (f32[10,128]{1,0:T(8,128)S(1)}, f32[2048,128]{1,0:T(8,128)S(1)}) custom-call(f32[2048,128]{1,0:T(8,128)S(1)} %get-tuple-element.34.pairs_ref, bf16[8,144,128]{2,1,0:T(8,128)(2,1)S(1)} %collective-permute-done.left_ref.before_ref, bf16[8,144,128]{2,1,0:T(8,128)(2,1)S(1)} %collective-permute-done.1.left_ref, bf16[8,8,16,256]{3,2,1,0:T(8,128)(2,1)S(1)} %bitcast.16, ...), custom_call_target="tpu_custom_call" | custom-call | flops 8589934592 | bytes 1048576 | tf_op jit(solution)/shard_map/second/pallas_call | solution.py:531
  42.2 1.2 %collective-permute-start.2 = (f32[16,128]{1,0:T(8,128)S(1)}, f32[16,128]{1,0:T(8,128)S(1)}, u32[]{:S(2)}, u32[]{:S(2)}) collective-permute-start(f32[16,128]{1,0:T(8,128)S(1)} %pad_maximum_fusion.1), channel_id=1, source_target_pairs={{0,7},{1,0},{2,1},{3,2},{4,3},{5,4},{6,5},{7,6},{8,15},{9,8},{10,9... | collective-permute-start | bytes 24584 | tf_op jit(solution)/shard_map/ppermute | solution.py:514
  43.4 3.4 %within.1 = (f32[16,128]{1,0:T(8,128)S(1)}, f32[16,128]{1,0:T(8,128)S(1)}) custom-call(bf16[16,144,128]{2,1,0:T(8,128)(2,1)S(1)} %all-to-all-done.got_ref, bf16[1024,2048]{1,0:T(8,128)(2,1)S(1)} %get-tuple-element.29.own_ref.ut_ref, bf16[2048,1024]{1,0:T(8,128)(2,1)S(1)} %get-tuple-element.30.u_ref, f32[2048,128]{1,0:T(8,128)S(1)} %get-tuple-element.31.slots_ref, ...), custom_call_target="tpu_custom_call" | custom-call | flops 4294967296 | bytes 1048576 | tf_op jit(solution)/shard_map/within/pallas_call | solution.py:536
  46.7 0.0 collective-permute-done.2
  46.8 11.2 %all_to_all.10.got_ref = f32[16,2,128]{2,1,0:T(2,128)S(1)} all-to-all(f32[16,2,128]{2,1,0:T(2,128)S(1)} %pad_maximum_fusion), channel_id=1, replica_groups=mesh['shard'=16,'blk'=8] {'shard'}, dimensions={0} | all-to-all | bytes 32768 | tf_op jit(solution)/shard_map/all_to_all | solution.py:559
  58.0 0.7 %pick.1 = (f32[8,128]{1,0:T(8,128)}, f32[8,128]{1,0:T(8,128)}) custom-call(f32[16,2,128]{2,1,0:T(2,128)S(1)} %all_to_all.10.got_ref, s32[8,128]{1,0:T(8,128)S(1)} %get-tuple-element.44.dest_ref, s32[8,128]{1,0:T(8,128)S(1)} %get-tuple-element.45.rank_ref), custom_call_target="tpu_custom_call" | custom-call | bytes 1048576 | tf_op jit(solution)/shard_map/pick/pallas_call | solution.py:560
  (4 shorter events, 0.1 us)
Async XLA Ops:
  4.0 19.9 %all-to-all-start = ((bf16[16,144,128]{2,1,0:T(8,128)(2,1)}), bf16[16,144,128]{2,1,0:T(8,128)(2,1)S(1)}, u32[]{:S(2)}, u32[]{:S(2)}) async-start(bf16[16,144,128]{2,1,0:T(8,128)(2,1)} %get-tuple-element.25), calls=%async_computation | async-start | bytes 1179648 | tf_op jit(solution)/shard_map/all_to_all | solution.py:551
  24.0 7.4 %collective-permute-start = (bf16[8,144,128]{2,1,0:T(8,128)(2,1)S(1)}, bf16[8,144,128]{2,1,0:T(8,128)(2,1)S(1)}, u32[]{:S(2)}, u32[]{:S(2)}) collective-permute-start(bf16[8,144,128]{2,1,0:T(8,128)(2,1)S(1)} %get-tuple-element.49), channel_id=1, source_target_pairs={{0,1},{1,2},{2,3},{3,4},{4,5},{5,6},{6,7},{7,0},{8,9},{9,10},{10,1... | collective-permute-start | bytes 884744 | tf_op jit(solution)/shard_map/ppermute | solution.py:514
  24.0 11.8 %collective-permute-start.1 = (bf16[8,144,128]{2,1,0:T(8,128)(2,1)S(1)}, bf16[8,144,128]{2,1,0:T(8,128)(2,1)S(1)}, u32[]{:S(2)}, u32[]{:S(2)}) collective-permute-start(bf16[8,144,128]{2,1,0:T(8,128)(2,1)S(1)} %get-tuple-element.48), channel_id=1, source_target_pairs={{0,1},{1,2},{2,3},{3,4},{4,5},{5,6},{6,7},{7,0},{8,9},{9,10},{10,1... | collective-permute-start | bytes 884744 | tf_op jit(solution)/shard_map/ppermute | solution.py:514
  42.2 4.6 %collective-permute-start.2 = (f32[16,128]{1,0:T(8,128)S(1)}, f32[16,128]{1,0:T(8,128)S(1)}, u32[]{:S(2)}, u32[]{:S(2)}) collective-permute-start(f32[16,128]{1,0:T(8,128)S(1)} %pad_maximum_fusion.1), channel_id=1, source_target_pairs={{0,7},{1,0},{2,1},{3,2},{4,3},{5,4},{6,5},{7,6},{8,15},{9,8},{10,9... | collective-permute-start | bytes 24584 | tf_op jit(solution)/shard_map/ppermute | solution.py:514
